TPU v7x, 256 devices: a whole 4x4x8 slice. The times are simulated.
256 devices in a mesh: exp: 64 (over z, x, core), head: 4 (over y).
Axes of the slice: x: 4, y: 4, z: 8, core: 2. Of those that a mesh axis runs over, the one named last changes fastest.
Arguments:
- queries: bfloat16 [8192, 4096], P('exp', 'head')
- keys: bfloat16 [8192, 1024], P('exp', 'head')
- values: bfloat16 [8192, 1024], P('exp', 'head')
- w_in: bfloat16 [64, 4096, 2, 768], P('exp', 'head'), may hold values from -0.09375 to 0.09375
- w_out: bfloat16 [64, 768, 4096], P('exp', None, 'head'), may hold values from -0.21875 to 0.21875
- routes: int32 [8192, 6], P('exp'), may hold values from 0 to 63, as said below
- route_weights: float32 [8192, 6], P('exp'), may hold values from 0.05 to 0.45
- grad_out: bfloat16 [8192, 4096], P('exp', 'head'), may hold values from -6 to 6
Outputs:
- output: bfloat16 [8192, 4096], P('exp', 'head')
- grad_attended: bfloat16 [8192, 4096], P('exp', 'head')
Inputs may be any that keep to these rules, and one draw needn't show every extreme that they name: `routes`: each row names 6 different experts. In each aligned block of 128 rows (the rows of one index of exp) no expert is named more than 14 times.
All inputs are finite; a program needn't handle non-finite values.
Results may differ from a plain program's by a relative error of at most 0.017.
Values may be sent and summed in bfloat16 or wider, within the bound.
No kernel may reach another device: no remote copies, remote signals or barrier semaphores. Data moves between devices by JAX's collectives and lax.ppermute only.
A program may use at most 128 MiB of HBM per device.

v0:
```python
import jax
import jax.numpy as jnp
from jax import lax
from jax.sharding import PartitionSpec as P

D = 4096
HEAD_WIDTH = 128
TOP = 6


norm_eps = 1e-05
hidden_logits = -1e30


def block_partial(query_rows, query_pos, rows_of_keys, value_rows, key_pos):
    row_count = query_rows.shape[0]
    count_of_blocks = rows_of_keys.shape[0]
    kv_heads = rows_of_keys.shape[2] // HEAD_WIDTH
    grouping_width = query_rows.shape[1] // HEAD_WIDTH // kv_heads
    heads_of_queries = query_rows.reshape(row_count, kv_heads, grouping_width, HEAD_WIDTH)
    key_heads = rows_of_keys.reshape(count_of_blocks, -1, kv_heads, HEAD_WIDTH)
    value_heads = value_rows.reshape(count_of_blocks, -1, kv_heads, HEAD_WIDTH)
    visible = (key_pos[:, None, :] <= query_pos[None, :, None])[:, :, None, None, :]
    scores = jnp.einsum(
        "tgid,bjgd->btgij", heads_of_queries, key_heads, preferred_element_type=jnp.float32
    ) * HEAD_WIDTH ** (-0.5)
    scores = jnp.where(visible, scores, hidden_logits)
    best_score = jnp.max(scores, axis=-1).astype(jnp.bfloat16)
    weights = jnp.where(visible, jnp.exp(scores - best_score.astype(jnp.float32)[..., None]), 0.0)
    weight_total = jnp.sum(weights, axis=-1).astype(jnp.bfloat16)
    weighted_sum = jnp.einsum(
        "btgij,bjgd->btgid",
        weights.astype(jnp.bfloat16),
        value_heads,
        preferred_element_type=jnp.float32,
    ).astype(jnp.bfloat16)
    head_count = kv_heads * grouping_width
    return (
        best_score.reshape(count_of_blocks, row_count, head_count),
        weight_total.reshape(count_of_blocks, row_count, head_count),
        weighted_sum.reshape(count_of_blocks, row_count, head_count * HEAD_WIDTH),
    )


def fold_partials(running, best_score, weight_total, weighted_sum):
    top_now, total_now, sums_now = running
    best_value = best_score.astype(jnp.float32)
    new_top = jnp.maximum(top_now, jnp.max(best_value, axis=0))
    old_factor = jnp.exp(top_now - new_top)
    block_factor = jnp.exp(best_value - new_top[None])
    total_next = total_now * old_factor + jnp.sum(
        weight_total.astype(jnp.float32) * block_factor, axis=0
    )
    spread_sums = weighted_sum.reshape(
        weighted_sum.shape[0], sums_now.shape[0], sums_now.shape[1], HEAD_WIDTH
    )
    sums_next = sums_now * old_factor[..., None] + jnp.sum(
        spread_sums.astype(jnp.float32) * block_factor[..., None], axis=0
    )
    return (new_top, total_next, sums_next)


def per_device(queries, keys, values, w_in, w_out, routes, route_weights, grad_out):
    exp_count = lax.axis_size("exp")
    exp_index = lax.axis_index("exp")
    token_count = queries.shape[0]
    query_width = queries.shape[1]
    head_count = query_width // HEAD_WIDTH
    cache_rows = keys.shape[0]
    window = token_count * exp_count
    offset = cache_rows * exp_count - window
    beginning = (
        jnp.full((token_count, head_count), hidden_logits, jnp.float32),
        jnp.zeros((token_count, head_count), jnp.float32),
        jnp.zeros((token_count, head_count, HEAD_WIDTH), jnp.float32),
    )
    own_pos = offset + exp_index * token_count + jnp.arange(token_count, dtype=jnp.int32)
    key_piece = lax.all_gather(keys, "exp", axis=0, tiled=True)
    value_piece = lax.all_gather(values, "exp", axis=0, tiled=True)
    piece_blocks = key_piece.shape[0] // cache_rows
    key_split = key_piece.reshape(piece_blocks, cache_rows, -1)
    value_split = value_piece.reshape(piece_blocks, cache_rows, -1)
    pos_split = jnp.arange(key_piece.shape[0], dtype=jnp.int32).reshape(piece_blocks, cache_rows)

    def one_block(state, element):
        key_block, value_block, pos_block = element
        block_parts = block_partial(
            queries, own_pos, key_block[None], value_block[None], pos_block[None]
        )
        return (fold_partials(state, block_parts[0], block_parts[1], block_parts[2]), None)

    state, ignored = lax.scan(one_block, beginning, (key_split, value_split, pos_split))
    attended = (
        (state[2] / state[1][..., None]).reshape(token_count, query_width).astype(jnp.bfloat16)
    )
    row_width = attended.shape[1]
    experts_all = w_in.shape[0] * exp_count
    mean_load = TOP * token_count // experts_all
    capacity = mean_load + mean_load // 6
    places = experts_all * capacity
    flat_routes = routes.reshape(-1)
    expert_hits = (
        flat_routes[:, None] == jnp.arange(experts_all, dtype=jnp.int32)[None, :]
    ).astype(jnp.int32)
    earlier = jnp.cumsum(expert_hits, axis=0) - expert_hits
    slot_index = jnp.sum(earlier * expert_hits, axis=1)
    place_index = flat_routes * capacity + slot_index
    chosen = (place_index[:, None] == jnp.arange(places, dtype=jnp.int32)[None, :]).astype(
        jnp.bfloat16
    )
    picker = jnp.sum(chosen.reshape(token_count, TOP, places), axis=1)
    contract_rows = (((0,), (0,)), ((), ()))
    send_rows = lax.dot_general(picker, attended, contract_rows, preferred_element_type=jnp.float32)
    send_rows = send_rows.astype(jnp.bfloat16).reshape(experts_all, capacity, row_width)
    send_grads = lax.dot_general(
        picker, grad_out, contract_rows, preferred_element_type=jnp.float32
    )
    send_grads = send_grads.astype(jnp.bfloat16).reshape(experts_all, capacity, row_width)
    w_first = w_in[0]
    w_second = w_out[0]
    rows_in = lax.all_to_all(send_rows, "exp", split_axis=0, concat_axis=0, tiled=True)
    grads_in = lax.all_to_all(send_grads, "exp", split_axis=0, concat_axis=0, tiled=True)
    lead_count, item_count, width_in = rows_in.shape
    row_total = lead_count * item_count
    row_block = rows_in.reshape(row_total, width_in)
    grad_block = grads_in.reshape(row_total, width_in)
    row_float = row_block.astype(jnp.float32)
    raw_sums = jnp.einsum("rd,dkf->rkf", row_block, w_first, preferred_element_type=jnp.float32)
    back_sums = lax.dot_general(
        grad_block, w_second, (((1,), (1,)), ((), ())), preferred_element_type=jnp.float32
    )
    squares = jnp.sum(row_float * row_float, axis=1)
    raw_sums, back_sums, squares = lax.psum((raw_sums, back_sums, squares), "head")
    norm_scale = lax.rsqrt(squares / D + norm_eps)[:, None]
    gate_value = raw_sums[:, 0] * norm_scale
    up_value = raw_sums[:, 1] * norm_scale
    gate_sigmoid = jax.nn.sigmoid(gate_value)
    gate_silu = gate_value * gate_sigmoid
    hidden_act = (gate_silu * up_value).astype(jnp.bfloat16)
    grad_gate = back_sums * up_value * gate_sigmoid * (1.0 + gate_value * (1.0 - gate_sigmoid))
    grad_up = back_sums * gate_silu
    grad_hidden = jnp.stack([grad_gate, grad_up], axis=1).astype(jnp.bfloat16)
    inner_sum = jnp.sum(
        grad_hidden.astype(jnp.float32) * jnp.stack([gate_value, up_value], axis=1), axis=(1, 2)
    )
    out_rows = jnp.dot(hidden_act, w_second, preferred_element_type=jnp.float32).astype(
        jnp.bfloat16
    )
    grad_normed = jnp.einsum(
        "rkf,dkf->rd", grad_hidden, w_first, preferred_element_type=jnp.float32
    )
    grad_rows = (
        norm_scale * grad_normed - row_float * (norm_scale * norm_scale / D) * inner_sum[:, None]
    )
    expert_out = out_rows.reshape(lead_count, item_count, width_in)
    expert_grad = grad_rows.astype(jnp.bfloat16).reshape(lead_count, item_count, width_in)
    came_out, came_grad = (
        lax.all_to_all(expert_out, "exp", split_axis=0, concat_axis=0, tiled=True),
        lax.all_to_all(expert_grad, "exp", split_axis=0, concat_axis=0, tiled=True),
    )
    picked_out = came_out.reshape(places, row_width)[place_index].reshape(
        token_count, TOP, row_width
    )
    picked_grad = came_grad.reshape(places, row_width)[place_index].reshape(
        token_count, TOP, row_width
    )
    output = attended.astype(jnp.float32) + jnp.sum(
        route_weights[:, :, None] * picked_out.astype(jnp.float32), axis=1
    )
    grad_attended = grad_out.astype(jnp.float32) + jnp.sum(
        route_weights[:, :, None] * picked_grad.astype(jnp.float32), axis=1
    )
    return (output.astype(jnp.bfloat16), grad_attended.astype(jnp.bfloat16))


def solution(mesh):
    in_specs = (
        P("exp", "head"),
        P("exp", "head"),
        P("exp", "head"),
        P("exp", "head", None, None),
        P("exp", None, "head"),
        P("exp", None),
        P("exp", None),
        P("exp", "head"),
    )
    out_specs = (P("exp", "head"), P("exp", "head"))
    return jax.shard_map(
        per_device, mesh=mesh, in_specs=in_specs, out_specs=out_specs, check_vma=False
    )
```

profile of v0, /device:TPU:2, one launch (start us, length us, event | category | flops | bytes accessed | tf_op | source)
XLA Modules:
  0.0 992.1 jit_solution(17389966856134589125)
XLA Ops:
  10.4 3.4 reduce-window.6
  16.3 2.9 convolution_convert_fusion.2
  19.2 3.8 reshape.260
  23.0 12.2 %all-to-all-start.2 = ((bf16[64,14,1024]{2,1,0:T(8,128)(2,1)}), bf16[64,14,1024]{2,1,0:T(8,128)(2,1)}, u32[]{:S(2)}, u32[]{:S(2)}) async-start(bf16[64,14,1024]{2,1,0:T(8,128)(2,1)} %reshape.260), calls=%async_computation.2 | async-start | bytes 4194304 | tf_op jit(solution)/shard_map/all_to_all | solution.py:122
  37.0 64.4 %all-gather.3.cloned.1.call-done = bf16[8192,256]{1,0:T(8,128)(2,1)} async-done(((bf16[128,256]{1,0:T(8,128)(2,1)}), bf16[8192,256]{1,0:T(8,128)(2,1)}) %all-gather.3.cloned.1.call-update) | async-done | bytes 4194320 | tf_op jit(solution)/shard_map/all_gather | solution.py:78
  101.4 79.3 %all-gather.5.cloned.1.call-done = bf16[8192,256]{1,0:T(8,128)(2,1)} async-done(((bf16[128,256]{1,0:T(8,128)(2,1)}), bf16[8192,256]{1,0:T(8,128)(2,1)}) %all-gather.5.cloned.1.call-update) | async-done | bytes 4194320 | tf_op jit(solution)/shard_map/all_gather | solution.py:79
  180.7 410.3 %while.16 = (s32[]{:T(128)}, f32[128,8]{0,1:T(8,128)}, f32[128,8]{0,1:T(8,128)}, f32[128,8,128]{0,2,1:T(8,128)}, s32[64,128]{1,0:T(8,128)}, /*index=5*/bf16[64,1...) while((s32[]{:T(128)}, f32[128,8]{0,1:T(8,128)}, ...), condition=%wide.wide.region_3.4_spmd.clone, body=%wide.wide.region_0.3_spmd.clone.sunk | while | flops 69099648 | bytes 8907468 | solution.py:92
  197.0 1.3 fusion.80
  222.7 1.3 fusion.80
  229.1 1.3 fusion.80
  235.5 1.3 fusion.80
  242.0 1.3 fusion.80
  261.2 1.3 fusion.80
  267.7 1.3 fusion.80
  274.1 1.3 fusion.80
  280.5 1.3 fusion.80
  312.6 1.3 fusion.80
  319.0 1.3 fusion.80
  592.1 2.9 convolution_convert_fusion.3
  595.0 3.8 reshape.256
  598.8 7.8 all-to-all-start
  606.7 3.8 reshape.261
  610.5 5.2 fusion.32
  615.7 42.1 %all-to-all-done = bf16[64,14,1024]{2,1,0:T(8,128)(2,1)} async-done(((bf16[64,14,1024]{2,1,0:T(8,128)(2,1)}), bf16[64,14,1024]{2,1,0:T(8,128)(2,1)}, u32[]{:S(2)}, u32[]{:S(2)}) %all-to-all-start) | async-done | bytes 1835040 | tf_op jit(solution)/shard_map/all_to_all | solution.py:121
  657.8 3.8 reshape.296
  661.6 6.4 fusion.23
  668.0 2.1 multiply_reduce_fusion.2
  670.3 3.8 reshape.257
  674.1 10.6 %psum.22 = f32[896]{0:T(1024)S(1)} all-reduce(f32[896]{0:T(1024)S(1)} %reduce_sum.84), channel_id=1, replica_groups=mesh['exp'=64,'head'=4] {'head'}, use_global_device_ids=true, to_apply=%region_10.11 | all-reduce | flops 896 | bytes 7168 | tf_op jit(solution)/shard_map/psum | solution.py:133
  684.6 143.3 %all-reduce.3.cloned.1.call-done = (f32[896,2,768]{2,0,1:T(8,128)}, f32[896,768]{1,0:T(8,128)}) async-done(((f32[896,2,768]{2,0,1:T(8,128)}, f32[896,768]{1,0:T(8,128)}), (f32[896,2,768]{2,0,1:T(8,128)}, f32[896,768]{1,0:T(8,128)})) %all-reduce.3.cloned.1.call-update) | async-done | bytes 8257552 | tf_op jit(solution)/shard_map/psum | solution.py:133
  827.9 3.2 slice_multiply_fusion.1
  832.3 2.7 copy-done.9
  835.0 1.8 fusion.38
  838.3 4.4 fusion.20
  842.8 3.8 reshape.262
  846.5 11.0 %all-to-all-start.3 = ((bf16[64,14,1024]{2,1,0:T(8,128)(2,1)}), bf16[64,14,1024]{2,1,0:T(8,128)(2,1)}, u32[]{:S(2)}, u32[]{:S(2)}) async-start(bf16[64,14,1024]{2,1,0:T(8,128)(2,1)} %reshape.262), calls=%async_computation.3 | async-start | bytes 4194304 | tf_op jit(solution)/shard_map/all_to_all | solution.py:159
  857.6 5.2 convolution_convert_fusion.1
  862.7 3.8 reshape.258
  866.5 42.2 %all-to-all-done.3 = bf16[64,14,1024]{2,1,0:T(8,128)(2,1)} async-done(((bf16[64,14,1024]{2,1,0:T(8,128)(2,1)}), bf16[64,14,1024]{2,1,0:T(8,128)(2,1)}, u32[]{:S(2)}, u32[]{:S(2)}) %all-to-all-start.3) | async-done | bytes 1835040 | tf_op jit(solution)/shard_map/all_to_all | solution.py:159
  908.7 5.6 all-to-all-start.1
  915.5 2.6 reshape.263
  918.1 3.5 gather_fusion.1
  921.7 43.8 %all-to-all-done.1 = bf16[64,14,1024]{2,1,0:T(8,128)(2,1)} async-done(((bf16[64,14,1024]{2,1,0:T(8,128)(2,1)}), bf16[64,14,1024]{2,1,0:T(8,128)(2,1)}, u32[]{:S(2)}, u32[]{:S(2)}) %all-to-all-start.1) | async-done | bytes 1835040 | tf_op jit(solution)/shard_map/all_to_all | solution.py:158
  965.5 2.6 reshape.259
  968.1 3.6 gather_fusion
  971.7 4.0 reshape.267
  975.7 2.2 reshape.268
  977.9 6.7 multiply_reduce_fusion
  (1077 shorter events, 405.5 us)
Async XLA Ops:
  7.2 654.4 %copy-start = (bf16[1,1024,2,768]{3,2,1,0:T(2,128)(2,1)S(1)}, bf16[1,1024,2,768]{3,2,1,0:T(2,128)(2,1)}, u32[]{:S(2)}) copy-start(bf16[1,1024,2,768]{3,2,1,0:T(2,128)(2,1)} %param.13) | copy-start | bytes 9437188
  7.2 94.2 %all-gather.3.cloned.1.call-start = ((), (), s32[]{:S(2)}) async-start(), calls=%async_computation.4 | async-start | bytes 4259840 | tf_op jit(solution)/shard_map/all_gather | solution.py:78
  7.9 172.8 %all-gather.5.cloned.1.call-start = ((), (), s32[]{:S(2)}) async-start(), calls=%async_computation.5 | async-start | bytes 4259840 | tf_op jit(solution)/shard_map/all_gather | solution.py:79
  14.3 8.7 copy-start.15
  23.0 575.8 %all-to-all-start.2 = ((bf16[64,14,1024]{2,1,0:T(8,128)(2,1)}), bf16[64,14,1024]{2,1,0:T(8,128)(2,1)}, u32[]{:S(2)}, u32[]{:S(2)}) async-start(bf16[64,14,1024]{2,1,0:T(8,128)(2,1)} %reshape.260), calls=%async_computation.2 | async-start | bytes 4194304 | tf_op jit(solution)/shard_map/all_to_all | solution.py:122
  189.0 2.9 copy-start.3
  285.4 2.9 copy-start.3
  291.8 2.9 copy-start.3
  298.2 2.9 copy-start.3
  304.6 2.9 copy-start.3
  311.0 2.9 copy-start.3
  317.4 2.9 copy-start.3
  323.9 2.9 copy-start.3
  336.7 2.9 copy-start.3
  349.5 2.9 copy-start.3
  362.3 2.9 copy-start.3
  375.2 2.9 copy-start.3
  445.7 2.9 copy-start.3
  465.0 2.9 copy-start.3
  484.3 2.9 copy-start.3
  497.1 2.9 copy-start.3
  510.0 2.9 copy-start.3
  522.8 2.9 copy-start.3
  535.7 2.9 copy-start.3
  542.1 2.9 copy-start.3
  548.5 2.9 copy-start.3
  555.0 2.9 copy-start.3
  561.4 2.9 copy-start.3
  567.8 2.9 copy-start.3
  574.2 2.9 copy-start.3
  580.7 2.9 copy-start.3
  587.1 2.9 copy-start.3
  598.8 59.0 %all-to-all-start = ((bf16[64,14,1024]{2,1,0:T(8,128)(2,1)}), bf16[64,14,1024]{2,1,0:T(8,128)(2,1)}, u32[]{:S(2)}, u32[]{:S(2)}) async-start(bf16[64,14,1024]{2,1,0:T(8,128)(2,1)} %reshape.256), calls=%async_computation | async-start | bytes 4194304 | tf_op jit(solution)/shard_map/all_to_all | solution.py:121
  606.6 221.3 %all-reduce.3.cloned.1.call-start = ((), (), s32[]{:S(2)}) async-start(), calls=%async_computation.6 | async-start | bytes 16515072 | tf_op jit(solution)/shard_map/psum | solution.py:133
  827.9 4.3 copy-start.2
  827.9 7.0 copy-start.9
  831.1 5.7 copy-start.5
  831.1 5.7 copy-start.7
  846.5 11.0 %copy-start.6 = (f32[896,1,768]{2,0,1:T(8,128)S(1)}, f32[896,1,768]{2,0,1:T(8,128)}, u32[]{:S(2)}) copy-start(f32[896,1,768]{2,0,1:T(8,128)} %copy-done.5) | copy-start | bytes 8257540
  846.5 62.2 %all-to-all-start.3 = ((bf16[64,14,1024]{2,1,0:T(8,128)(2,1)}), bf16[64,14,1024]{2,1,0:T(8,128)(2,1)}, u32[]{:S(2)}, u32[]{:S(2)}) async-start(bf16[64,14,1024]{2,1,0:T(8,128)(2,1)} %reshape.262), calls=%async_computation.3 | async-start | bytes 4194304 | tf_op jit(solution)/shard_map/all_to_all | solution.py:159
  866.5 47.8 %copy-start.17 = (f32[128,6]{0,1:T(8,128)S(1)}, f32[128,6]{0,1:T(8,128)}, u32[]{:S(2)}) copy-start(f32[128,6]{0,1:T(8,128)} %param.16) | copy-start | bytes 9220
  866.5 48.0 %copy-start.14 = (s32[128,6]{1,0:T(8,128)S(1)}, s32[128,6]{1,0:T(8,128)}, u32[]{:S(2)}) copy-start(s32[128,6]{1,0:T(8,128)} %get-tuple-element.146) | copy-start | bytes 9220
  866.5 48.1 %copy-start.16 = (s32[768]{0:T(1024)S(1)}, s32[768]{0:T(1024)}, u32[]{:S(2)}) copy-start(s32[768]{0:T(1024)} %copy-done.15) | copy-start | bytes 9220
  908.7 56.8 %all-to-all-start.1 = ((bf16[64,14,1024]{2,1,0:T(8,128)(2,1)}), bf16[64,14,1024]{2,1,0:T(8,128)(2,1)}, u32[]{:S(2)}, u32[]{:S(2)}) async-start(bf16[64,14,1024]{2,1,0:T(8,128)(2,1)} %reshape.258), calls=%async_computation.1 | async-start | bytes 4194304 | tf_op jit(solution)/shard_map/all_to_all | solution.py:158
  971.7 4.0 copy-start.8
  977.9 6.7 copy-start.12
  977.9 6.8 copy-start.13
  977.9 7.7 copy-start.1
  (103 other events, 160.6 us)
Sparse Core Ops, SparseCore 0:
  10.8 90.5 all-gather.2
  104.2 76.5 all-gather.4
  668.1 159.7 all-reduce.2
where the time goes:
time: 1000 us; the launch traced here: 992 us
  waiting for transfers between devices  416 us (42%)
  local copies, waits for them, and re-layouts  260 us (26%)
  other arithmetic  132 us (13%)
  matrix products  119 us (12%)
  starting transfers between devices  36.8 us (4%)
  between operations  14 us (1%)
  blocking collectives  10.6 us (1%)
    psum x1, waiting for transfers between devices, per_device(): lax.psum((raw_sums, back_sums, squares), 'head')  143 us
    dynamic_slice x192, local copies, waits for them, and re-layouts, per_device(): lax.scan(one_block, beginning, (key_split, value_split, pos_split))  110 us
    add x64, other arithmetic, fold_partials(): total_now * old_factor  82.7 us
    all_gather x1, waiting for transfers between devices, per_device(): value_piece = lax.all_gather(values, 'exp', axis=0, tiled=True)  79.3 us
    dot_general x64, matrix products, block_partial(): jnp.einsum('tgid,bjgd->btgij', heads_of_queries, key_heads, preferred_ele...  75.8 us
    all_gather x1, waiting for transfers between devices, per_device(): key_piece = lax.all_gather(keys, 'exp', axis=0, tiled=True)  64.4 us
    while x256, local copies, waits for them, and re-layouts  52.2 us
    all_to_all x1, waiting for transfers between devices, per_device(): lax.all_to_all(expert_out, 'exp', split_axis=0, concat_axis=0, tiled=True)  43.8 us
  transfers between devices with their start and end apart: 7, of which 6 were waited for; matrix products, arithmetic and copies ran while one was open for 41% of the time, Pallas kernels for 0%

commit v1 on v0

v1 whole, which is shorter than its diff:
```python
import functools

import jax
import jax.numpy as jnp
import numpy as np
from jax import lax
from jax.experimental import pallas as pl
from jax.experimental.pallas import tpu as pltpu
from jax.sharding import PartitionSpec as P

D = 4096
HEAD_WIDTH = 128
TOP = 6
norm_eps = 1e-05
hidden_logits = -1e30

ROWS = 128
HEADS = 8
GROUPS = 2
WIDTH = 1024
FF = 768
EXPERTS = 64
CAP = 14
PIECES = 4
PIECE = WIDTH // PIECES
BUNCH = 8
COMPACT = BUNCH * CAP
SPREAD = BUNCH * CAP * PIECES
BUNCHES = EXPERTS // BUNCH
PLACES = EXPERTS * CAP
F32 = jnp.float32
BF16 = jnp.bfloat16
MIB = 1 << 20


def params(mib):
    return pltpu.CompilerParams(vmem_limit_bytes=mib * MIB)


def spread_matrix():
    spread = np.arange(SPREAD)
    compact = np.arange(COMPACT)
    source = spread // (CAP * PIECES) * CAP + spread % CAP
    piece = spread % (CAP * PIECES) // CAP
    same = source[:, None] == compact[None, :]
    return np.stack([same & (piece[:, None] == j) for j in range(PIECES)]).astype(np.float32)


def dot(a, b):
    return lax.dot_general(a, b, (((1,), (0,)), ((), ())), preferred_element_type=F32)


def dot_t(a, b):
    return lax.dot_general(a, b, (((1,), (1,)), ((), ())), preferred_element_type=F32)


CHUNK = 8


def attention_kernel(place_ref, q_ref, kv_ref, o_ref, q_s, m_s, l_s, acc_s):
    step = pl.program_id(0)
    place = place_ref[0]
    per_group = HEADS // GROUPS
    rows = per_group * ROWS
    keys = CHUNK * ROWS
    factor = HEAD_WIDTH**-0.5 * 1.4426950408889634

    @pl.when(step == 0)
    def _():
        for i in range(HEADS):
            g, a = divmod(i, per_group)
            q_s[g, a * ROWS : (a + 1) * ROWS, :] = q_ref[:, i * HEAD_WIDTH : (i + 1) * HEAD_WIDTH]
        m_s[...] = jnp.full(m_s.shape, hidden_logits, F32)
        l_s[...] = jnp.zeros(l_s.shape, F32)
        acc_s[...] = jnp.zeros(acc_s.shape, F32)

    def update(masked):
        for g in range(GROUPS):
            k = kv_ref[:, g * HEAD_WIDTH : (g + 1) * HEAD_WIDTH]
            v = kv_ref[:, (GROUPS + g) * HEAD_WIDTH : (GROUPS + g + 1) * HEAD_WIDTH]
            s = dot_t(q_s[g], k)
            if masked:
                row = lax.broadcasted_iota(jnp.int32, (rows, keys), 0) & (ROWS - 1)
                col = lax.broadcasted_iota(jnp.int32, (rows, keys), 1) + (step * CHUNK - place) * ROWS
                s = jnp.where(col <= row, s, hidden_logits)
            best = s[:, :ROWS]
            for b in range(1, CHUNK):
                best = jnp.maximum(best, s[:, b * ROWS : (b + 1) * ROWS])
            m_old = m_s[g]
            m_new = jnp.maximum(m_old, jnp.max(best, axis=1, keepdims=True))
            decay = jnp.exp2((m_old - m_new) * factor)
            m_s[g] = m_new
            m_col = m_new[:, :1] * factor
            p = jnp.exp2(s * factor - m_col)
            total = p[:, :ROWS]
            for b in range(1, CHUNK):
                total = total + p[:, b * ROWS : (b + 1) * ROWS]
            l_s[g] = l_s[g] * decay + total
            acc_s[g] = acc_s[g] * decay + dot(p.astype(BF16), v)

    @pl.when((step + 1) * CHUNK <= place)
    def _():
        update(False)

    @pl.when(((step + 1) * CHUNK > place) & (step * CHUNK <= place))
    def _():
        update(True)

    @pl.when(step == pl.num_programs(0) - 1)
    def _():
        for i in range(HEADS):
            g, a = divmod(i, per_group)
            at = slice(a * ROWS, (a + 1) * ROWS)
            total = jnp.sum(l_s[g, at, :], axis=1, keepdims=True)
            o_ref[:, i * HEAD_WIDTH : (i + 1) * HEAD_WIDTH] = (acc_s[g, at, :] / total).astype(BF16)


def attention(place, queries, kv):
    steps = kv.shape[0] // (CHUNK * ROWS)
    rows = HEADS // GROUPS * ROWS
    keys = CHUNK * ROWS
    return pl.pallas_call(
        attention_kernel,
        grid_spec=pltpu.PrefetchScalarGridSpec(
            num_scalar_prefetch=1,
            grid=(steps,),
            in_specs=[
                pl.BlockSpec((ROWS, WIDTH), lambda i, s: (0, 0)),
                pl.BlockSpec((keys, kv.shape[1]), lambda i, s: (jnp.minimum(i, s[0] // CHUNK), 0)),
            ],
            out_specs=pl.BlockSpec((ROWS, WIDTH), lambda i, s: (0, 0)),
            scratch_shapes=[
                pltpu.VMEM((GROUPS, rows, HEAD_WIDTH), BF16),
                pltpu.VMEM((GROUPS, rows, HEAD_WIDTH), F32),
                pltpu.VMEM((GROUPS, rows, HEAD_WIDTH), F32),
                pltpu.VMEM((GROUPS, rows, HEAD_WIDTH), F32),
            ],
        ),
        out_shape=jax.ShapeDtypeStruct((ROWS, WIDTH), BF16),
        compiler_params=params(40),
        name="attention",
    )(place, queries, kv)


def pieces_of(values):
    return [values[:, j * PIECE : (j + 1) * PIECE] for j in range(PIECES)]


def send_kernel(picker_ref, rows_ref, spread_ref, o_ref):
    for b in range(BUNCHES):
        picked = dot(picker_ref[b * COMPACT : (b + 1) * COMPACT, :], rows_ref[...]).astype(BF16)
        out = sum(dot(spread_ref[j], part) for j, part in enumerate(pieces_of(picked)))
        o_ref[b * SPREAD : (b + 1) * SPREAD, :] = out.astype(BF16)


def send_rows(picker, rows, spread):
    return pl.pallas_call(
        send_kernel,
        out_shape=jax.ShapeDtypeStruct((PLACES * PIECES, PIECE), BF16),
        compiler_params=params(32),
        name="send_rows",
    )(picker, rows, spread)


def gather_compact(source_ref, gather_ref, target_ref):
    for b in range(BUNCHES):
        part = source_ref[b * SPREAD : (b + 1) * SPREAD, :]
        for j in range(PIECES):
            target_ref[b * COMPACT : (b + 1) * COMPACT, j * PIECE : (j + 1) * PIECE] = dot(
                gather_ref[j], part
            ).astype(BF16)


TILE = 256


def first_kernel(by_rows, x_ref, gather_ref, w_ref, o_ref, compact_ref):
    @pl.when(pl.program_id(0) == 0)
    def _():
        gather_compact(x_ref, gather_ref, compact_ref)

    product = dot_t if by_rows else dot
    o_ref[...] = product(compact_ref[...], w_ref[...]).astype(BF16)


def first_product(x, gather, w, by_rows):
    if by_rows:
        outs = w.shape[0]
        w_spec = pl.BlockSpec((TILE, WIDTH), lambda i: (i, 0))
    else:
        outs = w.shape[1]
        w_spec = pl.BlockSpec((WIDTH, TILE), lambda i: (0, i))
    return pl.pallas_call(
        functools.partial(first_kernel, by_rows),
        grid=(outs // TILE,),
        in_specs=[
            pl.BlockSpec(x.shape, lambda i: (0, 0)),
            pl.BlockSpec(gather.shape, lambda i: (0, 0, 0)),
            w_spec,
        ],
        out_specs=[
            pl.BlockSpec((PLACES, TILE), lambda i: (0, i)),
            pl.BlockSpec((PLACES, WIDTH), lambda i: (0, 0)),
        ],
        out_shape=[
            jax.ShapeDtypeStruct((PLACES, outs), BF16),
            jax.ShapeDtypeStruct((PLACES, WIDTH), BF16),
        ],
        compiler_params=params(40),
        name="first_product",
    )(x, gather, w)


def second_kernel(by_rows, corrected, *refs):
    if corrected:
        h_ref, w_ref, spread_ref, row_ref, weight_ref, o_ref, y_s = refs
    else:
        h_ref, w_ref, spread_ref, o_ref, y_s = refs
    step = pl.program_id(0)
    product = dot_t if by_rows else dot
    y = product(h_ref[...], w_ref[...])
    if corrected:
        y = y - row_ref[...].astype(F32) * weight_ref[...]
    y_s[step] = y.astype(BF16)

    @pl.when(step == PIECES - 1)
    def _():
        for b in range(BUNCHES):
            out = sum(
                dot(spread_ref[j], y_s[j, b * COMPACT : (b + 1) * COMPACT, :]) for j in range(PIECES)
            )
            o_ref[b * SPREAD : (b + 1) * SPREAD, :] = out.astype(BF16)


def second_product(h, w, spread, by_rows, rows=None, weight=None):
    depth = h.shape[1]
    w_spec = (
        pl.BlockSpec((PIECE, depth), lambda i: (i, 0))
        if by_rows
        else pl.BlockSpec((depth, PIECE), lambda i: (0, i))
    )
    in_specs = [
        pl.BlockSpec(h.shape, lambda i: (0, 0)),
        w_spec,
        pl.BlockSpec(spread.shape, lambda i: (0, 0, 0)),
    ]
    args = [h, w, spread]
    if rows is not None:
        in_specs += [
            pl.BlockSpec((PLACES, PIECE), lambda i: (0, i)),
            pl.BlockSpec((PLACES, 1), lambda i: (0, 0)),
        ]
        args += [rows, weight]
    return pl.pallas_call(
        functools.partial(second_kernel, by_rows, rows is not None),
        grid=(PIECES,),
        in_specs=in_specs,
        out_specs=pl.BlockSpec((PLACES * PIECES, PIECE), lambda i: (0, 0)),
        out_shape=jax.ShapeDtypeStruct((PLACES * PIECES, PIECE), BF16),
        scratch_shapes=[pltpu.VMEM((PIECES, PLACES, PIECE), BF16)],
        compiler_params=params(40),
        name="second_product",
    )(*args)


def combine_kernel(came_ref, gather_ref, weight_ref, base_ref, o_ref, compact_s):
    gather_compact(came_ref, gather_ref, compact_s)
    both = dot(weight_ref[...], compact_s[...])
    o_ref[...] = (base_ref[...].astype(F32) + (both[:ROWS] + both[ROWS:])).astype(BF16)


def combine(came, gather, weight, base):
    return pl.pallas_call(
        combine_kernel,
        out_shape=jax.ShapeDtypeStruct((ROWS, WIDTH), BF16),
        scratch_shapes=[pltpu.VMEM((PLACES, WIDTH), BF16)],
        compiler_params=params(32),
        name="combine",
    )(came, gather, weight, base)


def exchange(x):
    y = lax.all_to_all(
        x.reshape(EXPERTS, CAP * PIECES, PIECE), "exp", split_axis=0, concat_axis=0, tiled=True
    )
    return y.reshape(PLACES * PIECES, PIECE)


def head_sum(x):
    count = lax.axis_size("head")
    total = x
    for d in range(1, count):
        total = total + lax.ppermute(x, "head", [(i, (i + d) % count) for i in range(count)])
    return total


def per_device(queries, keys, values, w_in, w_out, routes, route_weights, grad_out):
    place = lax.axis_index("exp").astype(jnp.int32)
    head = lax.axis_index("head")
    w_first = w_in[0].reshape(WIDTH, 2 * FF)
    w_second = w_out[0]
    matrix = spread_matrix()
    spread = jnp.asarray(matrix, BF16)
    gather = jnp.asarray(matrix.transpose(0, 2, 1), BF16)

    kv = lax.all_gather(jnp.concatenate([keys, values], axis=1), "exp", axis=0, tiled=True)

    hits = routes[:, :, None] == jnp.arange(EXPERTS, dtype=jnp.int32)
    hit = jnp.any(hits, axis=1)
    earlier = jnp.asarray(np.tril(np.ones((ROWS, ROWS), np.float32), -1), BF16)
    rank = dot(earlier, hit.astype(BF16))
    rank = jnp.where(hit, rank, -1.0)
    token_weight = jnp.sum(jnp.where(hits, route_weights[:, :, None], 0.0), axis=1)
    slots = jnp.arange(CAP, dtype=jnp.int32).astype(F32)
    picker = (rank.T[:, None, :] == slots[None, :, None]).astype(BF16).reshape(PLACES, ROWS)
    weight = jnp.where(rank[:, :, None] == slots, token_weight[:, :, None], 0.0).reshape(ROWS, PLACES)
    weight_high = weight.astype(BF16)
    weight_low = (weight - weight_high.astype(F32)).astype(BF16)
    weight_both = jnp.concatenate([weight_high, weight_low], axis=0)

    grads_in = exchange(send_rows(picker, grad_out, spread))
    back, _ = first_product(grads_in, gather, w_second, True)
    back = lax.psum_scatter(back, "head", scatter_dimension=0, tiled=True).astype(F32)

    attended = attention(place[None], queries, kv)

    rows_in = exchange(send_rows(picker, attended, spread))
    raw, rows = first_product(rows_in, gather, w_first, False)
    raw = lax.psum_scatter(raw, "head", scatter_dimension=0, tiled=True).astype(F32)
    rows_float = rows.astype(F32)
    squares = head_sum(jnp.sum(rows_float * rows_float, axis=1))
    scale_all = lax.rsqrt(squares / D + norm_eps)
    quarter = PLACES // lax.axis_size("head")
    scale = lax.dynamic_slice_in_dim(scale_all, head * quarter, quarter)[:, None]
    gate = raw[:, :FF] * scale
    up = raw[:, FF:] * scale
    sigmoid = jax.nn.sigmoid(gate)
    silu = gate * sigmoid
    act = (silu * up).astype(BF16)
    grad_gate = (back * up * sigmoid * (1.0 + gate * (1.0 - sigmoid)) * scale).astype(BF16)
    grad_up = (back * silu * scale).astype(BF16)
    inner = jnp.sum(grad_gate.astype(F32) * gate + grad_up.astype(F32) * up, axis=1)
    correction = inner * scale[:, 0] / D
    act = lax.all_gather(act, "head", axis=0, tiled=True)
    grad_hidden = lax.all_gather(
        jnp.concatenate([grad_gate, grad_up], axis=1), "head", axis=0, tiled=True
    )
    correction = lax.all_gather(correction, "head", axis=0, tiled=True)[:, None]

    came_out = exchange(second_product(act, w_second, spread, False))
    came_grad = exchange(
        second_product(grad_hidden, w_first, spread, True, rows, correction)
    )
    output = combine(came_out, gather, weight_both, attended)
    grad_attended = combine(came_grad, gather, weight_both, grad_out)
    return (output, grad_attended)


def solution(mesh):
    in_specs = (
        P("exp", "head"),
        P("exp", "head"),
        P("exp", "head"),
        P("exp", "head", None, None),
        P("exp", None, "head"),
        P("exp", None),
        P("exp", None),
        P("exp", "head"),
    )
    out_specs = (P("exp", "head"), P("exp", "head"))
    return jax.shard_map(
        per_device, mesh=mesh, in_specs=in_specs, out_specs=out_specs, check_vma=False
    )
```

time: 1000 us -> 432 us (0.43)
  local copies, waits for them, and re-layouts: 260 us -> 29 us
  waiting for transfers between devices: 416 us -> 229 us
  other arithmetic: 132 us -> 12.2 us
  matrix products: 119 us -> 0.89 us
  blocking collectives: 10.6 us -> 60.7 us
  Pallas kernels: 0 us -> 39.7 us
    psum x1 -> x0, waiting for transfers between devices: 143 us -> none  [per_device(): lax.psum((raw_sums, back_sums, squares), 'head')]
    dot_general x134 -> x1, matrix products: 119 us -> 0.89 us  [dot(): lax.dot_general(a, b, (((1,), (0,)), ((), ())), preferred_element_type=F32)]
    dynamic_slice x192 -> x1, local copies, waits for them, and re-layouts: 110 us -> 0.08 us  [per_device(): lax.dynamic_slice_in_dim(scale_all, head * quarter, quarter)[:, None]]
    add x192 -> x0, other arithmetic: 96.1 us -> none  [the longest x64 82.7 us: fold_partials(): total_now * old_factor]
    while x256 -> x0, local copies, waits for them, and re-layouts: 52.2 us -> none
    all_to_all x0 -> x1, blocking collectives: none -> 51 us  [exchange(): lax.all_to_all(x.reshape(EXPERTS, CAP * PIECES, PIECE), 'exp', split_axis...]
    le x64 -> x0, local copies, waits for them, and re-layouts: 43.7 us -> none  [block_partial(): key_pos[:, None, :] <= query_pos[None, :, None]]
    pallas_call x0 -> x9, Pallas kernels: none -> 39.7 us  [the longest x2 11.5 us: first_product(): pl.pallas_call(functools.partial(first_kernel, by_rows), grid=(outs // TI...]
  transfers between devices with their start and end apart: 7 -> 11, of which waited for: 6 -> 9; matrix products, arithmetic and copies ran while one was open for 41% -> 3% of each run, Pallas kernels for 0% -> 5%
where the time goes in v1:
time: 432 us; the launch traced here: 431 us
  waiting for transfers between devices  229 us (53%)
  blocking collectives  60.7 us (14%)
  starting transfers between devices  44.7 us (10%)
  Pallas kernels  39.7 us (9%)
  local copies, waits for them, and re-layouts  29 us (7%)
  between operations  14.8 us (3%)
  other arithmetic  12.2 us (3%)
    all_to_all x3, waiting for transfers between devices, exchange(): lax.all_to_all(x.reshape(EXPERTS, CAP * PIECES, PIECE), 'exp', split_axis...  94.5 us
    all_gather x1, waiting for transfers between devices, per_device(): lax.all_gather(jnp.concatenate([keys, values], axis=1), 'exp', axis=0, ti...  85.2 us
    all_to_all x1, blocking collectives, exchange(): lax.all_to_all(x.reshape(EXPERTS, CAP * PIECES, PIECE), 'exp', split_axis...  51 us
    all_to_all x3, starting transfers between devices, exchange(): lax.all_to_all(x.reshape(EXPERTS, CAP * PIECES, PIECE), 'exp', split_axis...  39.8 us
    unnamed x57, local copies, waits for them, and re-layouts  27.2 us
    all_gather x1, waiting for transfers between devices, per_device(): act = lax.all_gather(act, 'head', axis=0, tiled=True)  25.5 us
    pallas_call x2, Pallas kernels, first_product(): pl.pallas_call(functools.partial(first_kernel, by_rows), grid=(outs // TI...  11.5 us
    reduce_scatter x1, waiting for transfers between devices, per_device(): lax.psum_scatter(back, 'head', scatter_dimension=0, tiled=True).astype(F32)  10.8 us
  transfers between devices with their start and end apart: 11, of which 9 were waited for; matrix products, arithmetic and copies ran while one was open for 3% of the time, Pallas kernels for 5%

profile of v1, /device:TPU:2, one launch (start us, length us, event | category | flops | bytes accessed | tf_op | source)
XLA Modules:
  0.0 430.9 jit_solution(11199717885314528318)
XLA Ops:
  7.2 1.6 pad_maximum_fusion.2
  9.7 0.9 bitcast_select_fusion.1
  10.9 85.2 %all-gather.4.cloned.1.call-done.kv_ref = bf16[8192,512]{1,0:T(8,128)(2,1)} async-done(((bf16[128,512]{1,0:T(8,128)(2,1)}), bf16[8192,512]{1,0:T(8,128)(2,1)}) %all-gather.4.cloned.1.call-update) | async-done | bytes 8388624 | tf_op jit(solution)/shard_map/all_gather | solution.py:306
  96.1 3.4 copy-done
  99.5 3.0 attention.1.rows_ref.base_ref
  102.4 4.1 send_rows.2
  106.5 23.4 %all-to-all-start = ((bf16[64,56,256]{2,1,0:T(8,128)(2,1)}), bf16[64,56,256]{2,1,0:T(8,128)(2,1)}, u32[]{:S(2)}, u32[]{:S(2)}) async-start(bf16[64,56,256]{2,1,0:T(8,128)(2,1)} %bitcast.2), calls=%async_computation | async-start | bytes 3670016 | tf_op jit(solution)/shard_map/all_to_all | solution.py:283
  129.9 2.5 copy.24
  132.4 43.1 %all-to-all-done = bf16[64,56,256]{2,1,0:T(8,128)(2,1)} async-done(((bf16[64,56,256]{2,1,0:T(8,128)(2,1)}), bf16[64,56,256]{2,1,0:T(8,128)(2,1)}, u32[]{:S(2)}, u32[]{:S(2)}) %all-to-all-start) | async-done | bytes 1835040 | tf_op jit(solution)/shard_map/all_to_all | solution.py:283
  175.5 1.0 copy-done.5
  176.5 6.9 %first_product.2 = (bf16[896,1536]{1,0:T(8,128)(2,1)S(1)}, bf16[896,1024]{1,0:T(8,128)(2,1)S(1)}) custom-call(bf16[3584,256]{1,0:T(8,128)(2,1)} %bitcast.3.x_ref, bf16[4,112,448]{2,1,0:T(8,128)(2,1)S(1)} %copy-done.5, bf16[1024,1536]{1,0:T(8,128)(2,1)S(1)} %bitcast.24), custom_call_target="tpu_custom_call" | custom-call | tf_op jit(solution)/shard_map/first_product/pallas_call | solution.py:193
  183.4 1.3 copy-done.1
  184.7 1.5 copy-done.15
  186.5 1.0 copy-done.9
  187.5 0.9 copy-done.17
  188.4 0.9 copy-done.21
  189.4 2.8 send_rows.3
  192.2 51.0 %all_to_all.20 = bf16[64,56,256]{2,1,0:T(8,128)(2,1)S(1)} all-to-all(bf16[64,56,256]{2,1,0:T(8,128)(2,1)S(1)} %bitcast.29), channel_id=1, replica_groups=mesh['exp'=64,'head'=4] {'exp'}, dimensions={0} | all-to-all | bytes 3670016 | tf_op jit(solution)/shard_map/all_to_all | solution.py:283
  243.2 4.6 %first_product.3 = (bf16[896,768]{1,0:T(8,128)(2,1)S(1)}, bf16[896,1024]{1,0:T(8,128)(2,1)}) custom-call(bf16[3584,256]{1,0:T(8,128)(2,1)S(1)} %bitcast.28, bf16[4,112,448]{2,1,0:T(8,128)(2,1)S(1)} %copy-done.6, bf16[768,1024]{1,0:T(8,128)(2,1)S(1)} %bitcast.30), custom_call_target="tpu_custom_call" | custom-call | tf_op jit(solution)/shard_map/first_product/pallas_call | solution.py:193
  247.9 1.1 copy-done.20
  249.0 1.9 multiply_reduce_fusion
  251.0 2.8 collective-permute-start.2
  255.5 3.4 collective-permute-done.1
  259.5 2.3 convert_element_type.53
  261.9 10.8 %reduce-scatter.5.cloned.1.call-done = bf16[224,768]{1,0:T(8,128)(2,1)} async-done(((bf16[896,768]{1,0:T(8,128)(2,1)}), bf16[224,768]{1,0:T(8,128)(2,1)}) %reduce-scatter.5.cloned.1.call-update) | async-done | bytes 344080 | tf_op jit(solution)/shard_map/reduce_scatter | solution.py:323
  272.7 3.0 add_reduce_fusion
  275.8 2.1 pad_maximum_fusion
  277.8 25.5 %all-gather.6.cloned.1.call-done.refs_0_ = bf16[896,768]{1,0:T(8,128)(2,1)} async-done(((bf16[224,768]{1,0:T(8,128)(2,1)}), bf16[896,768]{1,0:T(8,128)(2,1)}) %all-gather.6.cloned.1.call-update) | async-done | bytes 1376272 | tf_op jit(solution)/shard_map/all_gather | solution.py:344
  303.3 1.0 copy-done.10
  304.3 1.4 copy-done.13
  305.7 1.3 copy-done.19
  307.1 4.4 %second_product.2 = bf16[3584,256]{1,0:T(8,128)(2,1)S(1)} custom-call(bf16[896,768]{1,0:T(8,128)(2,1)S(1)} %copy-done.19, bf16[768,1024]{1,0:T(8,128)(2,1)S(1)} %bitcast.31, bf16[4,448,112]{2,1,0:T(8,128)(2,1)S(1)} %copy-done.10), custom_call_target="tpu_custom_call" | custom-call | tf_op jit(solution)/shard_map/second_product/pallas_call | solution.py:254
  311.5 1.3 copy-done.4
  312.8 10.8 %all-to-all-start.1 = ((bf16[64,56,256]{2,1,0:T(8,128)(2,1)}), bf16[64,56,256]{2,1,0:T(8,128)(2,1)}, u32[]{:S(2)}, u32[]{:S(2)}) async-start(bf16[64,56,256]{2,1,0:T(8,128)(2,1)} %bitcast.27), calls=%async_computation.2 | async-start | bytes 3670016 | tf_op jit(solution)/shard_map/all_to_all | solution.py:283
  325.1 9.7 %all-reduce = f32[896]{0:T(1024)S(1)} all-reduce(f32[896]{0:T(1024)S(1)} %multiply_dynamic-update-slice_fusion), channel_id=1, replica_groups=mesh['exp'=64,'head'=4] {'head'}, use_global_device_ids=true, to_apply=%add | all-reduce | flops 896 | bytes 7168
  334.8 1.0 broadcast_in_dim.56.refs_4_
  335.7 9.0 %all-gather.8.cloned.1.call-done.refs_0_ = bf16[896,1536]{1,0:T(8,128)(2,1)} async-done(((bf16[224,1536]{1,0:T(8,128)(2,1)}), bf16[896,1536]{1,0:T(8,128)(2,1)}) %all-gather.8.cloned.1.call-update) | async-done | bytes 2752528 | tf_op jit(solution)/shard_map/all_gather | solution.py:345
  344.7 1.5 copy-done.2
  346.2 1.0 copy-done.11
  347.3 1.8 copy-done.14
  349.0 1.0 copy-done.18
  350.1 6.0 %second_product.3 = bf16[3584,256]{1,0:T(8,128)(2,1)S(1)} custom-call(bf16[896,1536]{1,0:T(8,128)(2,1)S(1)} %copy-done.14, bf16[1024,1536]{1,0:T(8,128)(2,1)S(1)} %bitcast.25, bf16[4,448,112]{2,1,0:T(8,128)(2,1)S(1)} %copy-done.11, bf16[896,1024]{1,0:T(8,128)(2,1)S(1)} %copy-done.2, f32[896,1]{1,0:T(8,128)S(1)} %copy-done.18), custom_call_target="tpu_custom_call" | custom-call | tf_op jit(solution)/shard_map/second_product/pallas_call | solution.py:254
  356.1 1.3 copy-done.3
  357.3 11.9 %all-to-all-done.1 = bf16[64,56,256]{2,1,0:T(8,128)(2,1)} async-done(((bf16[64,56,256]{2,1,0:T(8,128)(2,1)}), bf16[64,56,256]{2,1,0:T(8,128)(2,1)}, u32[]{:S(2)}, u32[]{:S(2)}) %all-to-all-start.1) | async-done | bytes 1835040 | tf_op jit(solution)/shard_map/all_to_all | solution.py:283
  369.2 5.6 %all-to-all-start.3 = ((bf16[64,56,256]{2,1,0:T(8,128)(2,1)}), bf16[64,56,256]{2,1,0:T(8,128)(2,1)}, u32[]{:S(2)}, u32[]{:S(2)}) async-start(bf16[64,56,256]{2,1,0:T(8,128)(2,1)} %bitcast.26), calls=%async_computation.5 | async-start | bytes 3670016 | tf_op jit(solution)/shard_map/all_to_all | solution.py:283
  376.9 4.0 combine.2
  380.8 39.6 %all-to-all-done.3 = bf16[64,56,256]{2,1,0:T(8,128)(2,1)} async-done(((bf16[64,56,256]{2,1,0:T(8,128)(2,1)}), bf16[64,56,256]{2,1,0:T(8,128)(2,1)}, u32[]{:S(2)}, u32[]{:S(2)}) %all-to-all-start.3) | async-done | bytes 1835040 | tf_op jit(solution)/shard_map/all_to_all | solution.py:283
  420.4 4.0 combine.3
  (75 shorter events, 6.7 us)
Async XLA Ops:
  7.2 88.9 %copy-start.23 = (bf16[128,1024]{1,0:T(8,128)(2,1)S(1)}, bf16[128,1024]{1,0:T(8,128)(2,1)}, u32[]{:S(2)}) copy-start(bf16[128,1024]{1,0:T(8,128)(2,1)} %q_ref.1) | copy-start | bytes 786436
  7.2 88.9 %all-gather.4.cloned.1.call-start = ((), (), s32[]{:S(2)}) async-start(), calls=%async_computation.6 | async-start | bytes 8519680 | tf_op jit(solution)/shard_map/all_gather | solution.py:306
  10.9 91.5 %copy-start.16 = (bf16[896,128]{1,0:T(8,128)(2,1)}, bf16[896,128]{1,0:T(8,128)(2,1)S(1)}, u32[]{:S(2)}) copy-start(bf16[896,128]{1,0:T(8,128)(2,1)S(1)} %compare_convert_fusion.picker_ref) | copy-start | bytes 688132
  96.1 3.4 copy-start
  99.5 3.0 copy-start.8
  106.5 69.0 %all-to-all-start = ((bf16[64,56,256]{2,1,0:T(8,128)(2,1)}), bf16[64,56,256]{2,1,0:T(8,128)(2,1)}, u32[]{:S(2)}, u32[]{:S(2)}) async-start(bf16[64,56,256]{2,1,0:T(8,128)(2,1)} %bitcast.2), calls=%async_computation | async-start | bytes 3670016 | tf_op jit(solution)/shard_map/all_to_all | solution.py:283
  129.9 129.6 %reduce-scatter.3.cloned.1.call-start = ((), (), s32[]{:S(2)}) async-start(), calls=%async_computation.7 | async-start | bytes 3440640 | tf_op jit(solution)/shard_map/reduce_scatter | solution.py:329
  175.5 1.0 copy-start.5
  183.4 1.3 copy-start.1
  184.7 1.5 copy-start.15
  186.2 86.5 %reduce-scatter.5.cloned.1.call-start = ((), (), s32[]{:S(2)}) async-start(), calls=%async_computation.9 | async-start | bytes 1720320 | tf_op jit(solution)/shard_map/reduce_scatter | solution.py:323
  186.5 1.0 copy-start.9
  187.5 0.9 copy-start.17
  188.4 0.9 copy-start.21
  192.2 51.0 %copy-start.6 = (bf16[4,112,448]{2,1,0:T(8,128)(2,1)S(1)}, bf16[4,112,448]{2,1,0:T(8,128)(2,1)}, u32[]{:S(2)}) copy-start(bf16[4,112,448]{2,1,0:T(8,128)(2,1)} %constant.37.clone.gather_ref) | copy-start | bytes 1204228
  192.2 51.0 %copy-start.12 = (bf16[1,768,1024]{2,1,0:T(8,128)(2,1)S(1)}, bf16[1,768,1024]{2,1,0:T(8,128)(2,1)}, u32[]{:S(2)}) copy-start(bf16[1,768,1024]{2,1,0:T(8,128)(2,1)} %param.15) | copy-start | bytes 4718596
  247.9 1.1 copy-start.20
  249.0 54.3 %all-gather.6.cloned.1.call-start = ((), (), s32[]{:S(2)}) async-start(), calls=%async_computation.8 | async-start | bytes 1720320 | tf_op jit(solution)/shard_map/all_gather | solution.py:344
  251.0 4.5 %collective-permute-start.2 = (f32[896]{0:T(1024)S(1)}, f32[896]{0:T(1024)S(1)}, u32[]{:S(2)}, u32[]{:S(2)}) collective-permute-start(f32[896]{0:T(1024)S(1)} %multiply_reduce_fusion), channel_id=1, source_target_pairs={{0,3},{1,0},{2,1},{3,2},{4,7},{5,4},{6,5},{7,6},{8,11},{9,8},{10,9... | collective-permute-start | bytes 10760 | tf_op jit(solution)/shard_map/ppermute | solution.py:293
  253.8 5.1 %collective-permute-start.1 = (f32[896]{0:T(1024)S(1)}, f32[896]{0:T(1024)S(1)}, u32[]{:S(2)}, u32[]{:S(2)}) collective-permute-start(f32[896]{0:T(1024)S(1)} %multiply_reduce_fusion), channel_id=1, source_target_pairs={{0,2},{1,3},{2,0},{3,1},{4,6},{5,7},{6,4},{7,5},{8,10},{9,11},{10,... | collective-permute-start | bytes 10760 | tf_op jit(solution)/shard_map/ppermute | solution.py:293
  254.6 4.8 %collective-permute-start = (f32[896]{0:T(1024)S(1)}, f32[896]{0:T(1024)S(1)}, u32[]{:S(2)}, u32[]{:S(2)}) collective-permute-start(f32[896]{0:T(1024)S(1)} %multiply_reduce_fusion), channel_id=1, source_target_pairs={{0,1},{1,2},{2,3},{3,0},{4,5},{5,6},{6,7},{7,4},{8,9},{9,10},{10,1... | collective-permute-start | bytes 10760 | tf_op jit(solution)/shard_map/ppermute | solution.py:293
  275.7 69.0 %all-gather.8.cloned.1.call-start = ((), (), s32[]{:S(2)}) async-start(), calls=%async_computation.10 | async-start | bytes 3440640 | tf_op jit(solution)/shard_map/all_gather | solution.py:345
  303.3 1.0 copy-start.10
  304.3 1.4 copy-start.13
  305.7 1.3 copy-start.19
  311.5 1.3 copy-start.4
  312.8 10.9 %copy-start.26 = (u32[256]{0:T(256)S(1)}, u32[256]{0:T(256)}, u32[]{:S(2)}) copy-start(u32[256]{0:T(256)} %constant.43) | copy-start | bytes 3076
  312.8 56.4 %all-to-all-start.1 = ((bf16[64,56,256]{2,1,0:T(8,128)(2,1)}), bf16[64,56,256]{2,1,0:T(8,128)(2,1)}, u32[]{:S(2)}, u32[]{:S(2)}) async-start(bf16[64,56,256]{2,1,0:T(8,128)(2,1)} %bitcast.27), calls=%async_computation.2 | async-start | bytes 3670016 | tf_op jit(solution)/shard_map/all_to_all | solution.py:283
  344.7 1.5 copy-start.2
  346.2 1.0 copy-start.11
  347.3 1.8 copy-start.14
  349.0 1.0 copy-start.18
  356.1 1.3 copy-start.3
  369.2 51.2 %all-to-all-start.3 = ((bf16[64,56,256]{2,1,0:T(8,128)(2,1)}), bf16[64,56,256]{2,1,0:T(8,128)(2,1)}, u32[]{:S(2)}, u32[]{:S(2)}) async-start(bf16[64,56,256]{2,1,0:T(8,128)(2,1)} %bitcast.26), calls=%async_computation.5 | async-start | bytes 3670016 | tf_op jit(solution)/shard_map/all_to_all | solution.py:283
  374.8 0.7 copy-start.24
  374.8 0.7 copy-start.25
  375.9 1.0 copy-start.7
  376.0 44.4 %copy-start.22 = (bf16[128,1024]{1,0:T(8,128)(2,1)S(1)}, bf16[128,1024]{1,0:T(8,128)(2,1)}, u32[]{:S(2)}) copy-start(bf16[128,1024]{1,0:T(8,128)(2,1)} %base_ref.1) | copy-start | bytes 786436
Sparse Core Ops, SparseCore 0:
  11.4 84.6 all-gather.3
  186.4 33.7 reduce-scatter.2
  249.1 23.5 reduce-scatter.4
  275.8 27.4 all-gather.5
  305.1 39.6 all-gather.7

commit v2 on v1

--- a/solution.py
+++ b/solution.py
@@ -20,6 +20,7 @@
 WIDTH = 1024
 FF = 768
 EXPERTS = 64
+HEAD_COUNT = 4
 CAP = 14
 PIECES = 4
 PIECE = WIDTH // PIECES
@@ -157,7 +158,7 @@
     return pl.pallas_call(
         send_kernel,
         out_shape=jax.ShapeDtypeStruct((PLACES * PIECES, PIECE), BF16),
-        compiler_params=params(32),
+        compiler_params=params(14),
         name="send_rows",
     )(picker, rows, spread)
 
@@ -174,10 +175,21 @@
 TILE = 256
 
 
-def first_kernel(by_rows, x_ref, gather_ref, w_ref, o_ref, compact_ref):
+def high_low(x):
+    high = x.astype(BF16).astype(F32)
+    column = lax.broadcasted_iota(jnp.int32, (x.shape[0], 128), 1)
+    return jnp.where(column == 0, high, jnp.where(column == 1, x - high, 0.0)).astype(BF16)
+
+
+def first_kernel(by_rows, x_ref, gather_ref, w_ref, o_ref, compact_ref, squares_ref):
     @pl.when(pl.program_id(0) == 0)
     def _():
         gather_compact(x_ref, gather_ref, compact_ref)
+        for b in range(BUNCHES):
+            rows = compact_ref[b * COMPACT : (b + 1) * COMPACT, :].astype(F32)
+            squares_ref[b * COMPACT : (b + 1) * COMPACT, :] = high_low(
+                jnp.sum(rows * rows, axis=1, keepdims=True)
+            )
 
     product = dot_t if by_rows else dot
     o_ref[...] = product(compact_ref[...], w_ref[...]).astype(BF16)
@@ -201,26 +213,41 @@
         out_specs=[
             pl.BlockSpec((PLACES, TILE), lambda i: (0, i)),
             pl.BlockSpec((PLACES, WIDTH), lambda i: (0, 0)),
+            pl.BlockSpec((PLACES, 128), lambda i: (0, 0)),
         ],
         out_shape=[
             jax.ShapeDtypeStruct((PLACES, outs), BF16),
             jax.ShapeDtypeStruct((PLACES, WIDTH), BF16),
+            jax.ShapeDtypeStruct((PLACES, 128), BF16),
         ],
-        compiler_params=params(40),
+        compiler_params=params(22),
         name="first_product",
     )(x, gather, w)
 
 
-def second_kernel(by_rows, corrected, *refs):
+def second_kernel(by_rows, corrected, head_ref, *refs):
+    pieces, refs = refs[:HEAD_COUNT], refs[HEAD_COUNT:]
     if corrected:
-        h_ref, w_ref, spread_ref, row_ref, weight_ref, o_ref, y_s = refs
+        w_ref, spread_ref, row_ref, o_ref, h_s, y_s, weight_s = refs
     else:
-        h_ref, w_ref, spread_ref, o_ref, y_s = refs
+        w_ref, spread_ref, o_ref, h_s, y_s = refs
     step = pl.program_id(0)
+    depth = h_s.shape[1]
+    quarter = PLACES // HEAD_COUNT
+
+    @pl.when(step == 0)
+    def _():
+        for d, piece in enumerate(pieces):
+            at = lax.rem(head_ref[0] + d, HEAD_COUNT) * quarter
+            at = pl.ds(pl.multiple_of(at, 16), quarter)
+            h_s[at, :] = piece[:, :depth]
+            if corrected:
+                weight_s[at, :] = piece[:, depth : depth + 128].astype(F32)
+
     product = dot_t if by_rows else dot
-    y = product(h_ref[...], w_ref[...])
+    y = product(h_s[...], w_ref[...])
     if corrected:
-        y = y - row_ref[...].astype(F32) * weight_ref[...]
+        y = y - row_ref[...].astype(F32) * (weight_s[:, 0:1] + weight_s[:, 1:2])
     y_s[step] = y.astype(BF16)
 
     @pl.when(step == PIECES - 1)
@@ -232,35 +259,36 @@
             o_ref[b * SPREAD : (b + 1) * SPREAD, :] = out.astype(BF16)
 
 
-def second_product(h, w, spread, by_rows, rows=None, weight=None):
-    depth = h.shape[1]
+def second_product(head, pieces, w, spread, by_rows, rows=None):
+    depth = w.shape[1] if by_rows else w.shape[0]
     w_spec = (
-        pl.BlockSpec((PIECE, depth), lambda i: (i, 0))
+        pl.BlockSpec((PIECE, depth), lambda i, s: (i, 0))
         if by_rows
-        else pl.BlockSpec((depth, PIECE), lambda i: (0, i))
+        else pl.BlockSpec((depth, PIECE), lambda i, s: (0, i))
     )
-    in_specs = [
-        pl.BlockSpec(h.shape, lambda i: (0, 0)),
+    in_specs = [pl.BlockSpec(piece.shape, lambda i, s: (0, 0)) for piece in pieces] + [
         w_spec,
-        pl.BlockSpec(spread.shape, lambda i: (0, 0, 0)),
+        pl.BlockSpec(spread.shape, lambda i, s: (0, 0, 0)),
     ]
-    args = [h, w, spread]
+    args = [*pieces, w, spread]
+    scratch = [pltpu.VMEM((PLACES, depth), BF16), pltpu.VMEM((PIECES, PLACES, PIECE), BF16)]
     if rows is not None:
-        in_specs += [
-            pl.BlockSpec((PLACES, PIECE), lambda i: (0, i)),
-            pl.BlockSpec((PLACES, 1), lambda i: (0, 0)),
-        ]
-        args += [rows, weight]
+        in_specs += [pl.BlockSpec((PLACES, PIECE), lambda i, s: (0, i))]
+        args += [rows]
+        scratch += [pltpu.VMEM((PLACES, 128), F32)]
     return pl.pallas_call(
         functools.partial(second_kernel, by_rows, rows is not None),
-        grid=(PIECES,),
-        in_specs=in_specs,
-        out_specs=pl.BlockSpec((PLACES * PIECES, PIECE), lambda i: (0, 0)),
+        grid_spec=pltpu.PrefetchScalarGridSpec(
+            num_scalar_prefetch=1,
+            grid=(PIECES,),
+            in_specs=in_specs,
+            out_specs=pl.BlockSpec((PLACES * PIECES, PIECE), lambda i, s: (0, 0)),
+            scratch_shapes=scratch,
+        ),
         out_shape=jax.ShapeDtypeStruct((PLACES * PIECES, PIECE), BF16),
-        scratch_shapes=[pltpu.VMEM((PIECES, PLACES, PIECE), BF16)],
-        compiler_params=params(40),
+        compiler_params=params(32),
         name="second_product",
-    )(*args)
+    )(head[None], *args)
 
 
 def combine_kernel(came_ref, gather_ref, weight_ref, base_ref, o_ref, compact_s):
@@ -274,7 +302,7 @@
         combine_kernel,
         out_shape=jax.ShapeDtypeStruct((ROWS, WIDTH), BF16),
         scratch_shapes=[pltpu.VMEM((PLACES, WIDTH), BF16)],
-        compiler_params=params(32),
+        compiler_params=params(18),
         name="combine",
     )(came, gather, weight, base)
 
@@ -286,24 +314,39 @@
     return y.reshape(PLACES * PIECES, PIECE)
 
 
-def head_sum(x):
-    count = lax.axis_size("head")
-    total = x
-    for d in range(1, count):
-        total = total + lax.ppermute(x, "head", [(i, (i + d) % count) for i in range(count)])
-    return total
+def from_head(x, d):
+    return lax.ppermute(x, "head", [((i + d) % HEAD_COUNT, i) for i in range(HEAD_COUNT)])
+
+
+OTHERS = (1, 3, 2)
+
+
+def head_scatter(head, x):
+    rows = x.shape[0] // HEAD_COUNT
+
+    def part(d):
+        return lax.dynamic_slice_in_dim(x, (head + d) % HEAD_COUNT * rows, rows)
+
+    return [part(0)] + [from_head(part(-d), d) for d in OTHERS]
+
+
+def head_gather(x):
+    parts = {d: from_head(x, d) for d in OTHERS}
+    return [x] + [parts[d] for d in range(1, HEAD_COUNT)]
+
+
+def total(parts):
+    return functools.reduce(jnp.add, [part.astype(F32) for part in parts])
 
 
 def per_device(queries, keys, values, w_in, w_out, routes, route_weights, grad_out):
     place = lax.axis_index("exp").astype(jnp.int32)
-    head = lax.axis_index("head")
+    head = lax.axis_index("head").astype(jnp.int32)
     w_first = w_in[0].reshape(WIDTH, 2 * FF)
     w_second = w_out[0]
     matrix = spread_matrix()
     spread = jnp.asarray(matrix, BF16)
     gather = jnp.asarray(matrix.transpose(0, 2, 1), BF16)
-
-    kv = lax.all_gather(jnp.concatenate([keys, values], axis=1), "exp", axis=0, tiled=True)
 
     hits = routes[:, :, None] == jnp.arange(EXPERTS, dtype=jnp.int32)
     hit = jnp.any(hits, axis=1)
@@ -318,39 +361,37 @@
     weight_low = (weight - weight_high.astype(F32)).astype(BF16)
     weight_both = jnp.concatenate([weight_high, weight_low], axis=0)
 
+    kv = lax.all_gather(jnp.concatenate([keys, values], axis=1), "exp", axis=0, tiled=True)
     grads_in = exchange(send_rows(picker, grad_out, spread))
-    back, _ = first_product(grads_in, gather, w_second, True)
-    back = lax.psum_scatter(back, "head", scatter_dimension=0, tiled=True).astype(F32)
-
+    back, _, _ = first_product(grads_in, gather, w_second, True)
+    back = head_scatter(head, back)
+    kv, weight_both, *back = lax.optimization_barrier((kv, weight_both, *back))
     attended = attention(place[None], queries, kv)
 
     rows_in = exchange(send_rows(picker, attended, spread))
-    raw, rows = first_product(rows_in, gather, w_first, False)
-    raw = lax.psum_scatter(raw, "head", scatter_dimension=0, tiled=True).astype(F32)
-    rows_float = rows.astype(F32)
-    squares = head_sum(jnp.sum(rows_float * rows_float, axis=1))
-    scale_all = lax.rsqrt(squares / D + norm_eps)
-    quarter = PLACES // lax.axis_size("head")
-    scale = lax.dynamic_slice_in_dim(scale_all, head * quarter, quarter)[:, None]
+    raw, rows, squares = first_product(rows_in, gather, w_first, False)
+    raw = head_scatter(head, jnp.concatenate([raw, squares], axis=1))
+    raw = total(raw)
+    squares = raw[:, 2 * FF : 2 * FF + 1] + raw[:, 2 * FF + 1 : 2 * FF + 2]
+    scale = lax.rsqrt(squares / D + norm_eps)
     gate = raw[:, :FF] * scale
-    up = raw[:, FF:] * scale
+    lift = raw[:, FF : 2 * FF] * scale
     sigmoid = jax.nn.sigmoid(gate)
     silu = gate * sigmoid
-    act = (silu * up).astype(BF16)
-    grad_gate = (back * up * sigmoid * (1.0 + gate * (1.0 - sigmoid)) * scale).astype(BF16)
+    act = (silu * lift).astype(BF16)
+    gathered = head_gather(act)
+    back = total(back)
+    grad_gate = (back * lift * sigmoid * (1.0 + gate * (1.0 - sigmoid)) * scale).astype(BF16)
     grad_up = (back * silu * scale).astype(BF16)
-    inner = jnp.sum(grad_gate.astype(F32) * gate + grad_up.astype(F32) * up, axis=1)
-    correction = inner * scale[:, 0] / D
-    act = lax.all_gather(act, "head", axis=0, tiled=True)
-    grad_hidden = lax.all_gather(
-        jnp.concatenate([grad_gate, grad_up], axis=1), "head", axis=0, tiled=True
+    inner = jnp.sum(
+        grad_gate.astype(F32) * gate + grad_up.astype(F32) * lift, axis=1, keepdims=True
     )
-    correction = lax.all_gather(correction, "head", axis=0, tiled=True)[:, None]
-
-    came_out = exchange(second_product(act, w_second, spread, False))
-    came_grad = exchange(
-        second_product(grad_hidden, w_first, spread, True, rows, correction)
-    )
+    correction = high_low(inner * scale / D)
+    grad_hidden = jnp.concatenate([grad_gate, grad_up, correction], axis=1)
+    grad_hidden, *gathered = lax.optimization_barrier((grad_hidden, *gathered))
+    came_out = exchange(second_product(head, gathered, w_second, spread, False))
+    grad_hidden = head_gather(grad_hidden)
+    came_grad = exchange(second_product(head, grad_hidden, w_first, spread, True, rows))
     output = combine(came_out, gather, weight_both, attended)
     grad_attended = combine(came_grad, gather, weight_both, grad_out)
     return (output, grad_attended)

time: 432 us -> 380 us (0.88)
  blocking collectives: 60.7 us -> 0 us
  starting transfers between devices: 44.7 us -> 66.9 us
  waiting for transfers between devices: 229 us -> 219 us
    ppermute x3 -> x12, waiting for transfers between devices: 3.94 us -> 90 us  [from_head(): lax.ppermute(x, 'head', [((i + d) % HEAD_COUNT, i) for i in range(HEAD_CO...]
    all_gather x1, waiting for transfers between devices: 85.2 us -> 0.01 us  [per_device(): lax.all_gather(jnp.concatenate([keys, values], axis=1), 'exp', axis=0, ti...]
    all_to_all x1 -> x0, blocking collectives: 51 us -> none  [exchange(): lax.all_to_all(x.reshape(EXPERTS, CAP * PIECES, PIECE), 'exp', split_axis...]
    all_gather x2 -> x0, waiting for transfers between devices: 34.5 us -> none  [the longest x1 25.5 us: per_device(): act = lax.all_gather(act, 'head', axis=0, tiled=True)]
    all_to_all x3 -> x4, waiting for transfers between devices: 94.5 us -> 129 us  [exchange(): lax.all_to_all(x.reshape(EXPERTS, CAP * PIECES, PIECE), 'exp', split_axis...]
    all_to_all x3 -> x4, starting transfers between devices: 39.8 us -> 51.8 us  [exchange(): lax.all_to_all(x.reshape(EXPERTS, CAP * PIECES, PIECE), 'exp', split_axis...]
    reduce_scatter x2 -> x0, waiting for transfers between devices: 10.8 us -> none  [the longest x1 10.8 us: per_device(): lax.psum_scatter(back, 'head', scatter_dimension=0, tiled=True).astype(F32)]
    ppermute x3 -> x12, starting transfers between devices: 4.5 us -> 15.1 us  [from_head(): lax.ppermute(x, 'head', [((i + d) % HEAD_COUNT, i) for i in range(HEAD_CO...]
  transfers between devices with their start and end apart: 11 -> 17, of which waited for: 9 -> 11; matrix products, arithmetic and copies ran while one was open for 3% -> 4% of each run, Pallas kernels for 5% -> 5%
where the time goes in v2:
time: 380 us; the launch traced here: 379 us
  waiting for transfers between devices  219 us (58%)
  starting transfers between devices  66.9 us (18%)
  Pallas kernels  40 us (11%)
  local copies, waits for them, and re-layouts  25.9 us (7%)
  between operations  14.5 us (4%)
  other arithmetic  12 us (3%)
    all_to_all x4, waiting for transfers between devices, exchange(): lax.all_to_all(x.reshape(EXPERTS, CAP * PIECES, PIECE), 'exp', split_axis...  129 us
    ppermute x12, waiting for transfers between devices, from_head(): lax.ppermute(x, 'head', [((i + d) % HEAD_COUNT, i) for i in range(HEAD_CO...  90 us
    all_to_all x4, starting transfers between devices, exchange(): lax.all_to_all(x.reshape(EXPERTS, CAP * PIECES, PIECE), 'exp', split_axis...  51.8 us
    unnamed x60, local copies, waits for them, and re-layouts  19.5 us
    ppermute x12, starting transfers between devices, from_head(): lax.ppermute(x, 'head', [((i + d) % HEAD_COUNT, i) for i in range(HEAD_CO...  15.1 us
    pallas_call x2, Pallas kernels, second_product(): pl.pallas_call(functools.partial(second_kernel, by_rows, rows is not None...  12 us
    pallas_call x2, Pallas kernels, first_product(): pl.pallas_call(functools.partial(first_kernel, by_rows), grid=(outs // TI...  11.7 us
  transfers between devices with their start and end apart: 17, of which 11 were waited for; matrix products, arithmetic and copies ran while one was open for 4% of the time, Pallas kernels for 5%

profile of v2, /device:TPU:2, one launch (start us, length us, event | category | flops | bytes accessed | tf_op | source)
XLA Modules:
  0.0 379.1 jit_solution(9283716416981523167)
XLA Ops:
  7.2 1.6 pad_maximum_fusion.2
  10.9 2.8 send_rows.2
  13.8 1.3 copy-done.2
  15.0 12.0 %all-to-all-start = ((bf16[64,56,256]{2,1,0:T(8,128)(2,1)}), bf16[64,56,256]{2,1,0:T(8,128)(2,1)S(1)}, u32[]{:S(2)}, u32[]{:S(2)}) async-start(bf16[64,56,256]{2,1,0:T(8,128)(2,1)} %bitcast.30), calls=%async_computation | async-start | bytes 3670016 | tf_op jit(solution)/shard_map/all_to_all | solution.py:311
  28.6 1.9 broadcast_in_dim.79
  30.5 2.0 copy.25
  32.5 1.8 fusion.2
  34.3 44.2 %all-to-all-done = bf16[64,56,256]{2,1,0:T(8,128)(2,1)S(1)} async-done(((bf16[64,56,256]{2,1,0:T(8,128)(2,1)}), bf16[64,56,256]{2,1,0:T(8,128)(2,1)S(1)}, u32[]{:S(2)}, u32[]{:S(2)}) %all-to-all-start) | async-done | bytes 1835040 | tf_op jit(solution)/shard_map/all_to_all | solution.py:311
  78.5 1.4 copy-done.10
  79.9 4.7 %first_product.2 = (bf16[896,768]{1,0:T(8,128)(2,1)S(1)}, bf16[896,1024]{1,0:T(8,128)(2,1)}, bf16[896,128]{1,0:T(8,128)(2,1)}) custom-call(bf16[3584,256]{1,0:T(8,128)(2,1)S(1)} %bitcast.29, bf16[4,112,448]{2,1,0:T(8,128)(2,1)S(1)} %copy-done.4, bf16[768,1024]{1,0:T(8,128)(2,1)S(1)} %bitcast.32), custom_call_target="tpu_custom_call" | custom-call | tf_op jit(solution)/shard_map/first_product/pallas_call | solution.py:205
  85.5 2.8 collective-permute-start
  88.3 2.3 collective-permute-start.2
  91.5 11.2 %collective-permute-done = bf16[224,768]{1,0:T(8,128)(2,1)S(1)} collective-permute-done((bf16[224,768]{1,0:T(8,128)(2,1)S(1)}, bf16[224,768]{1,0:T(8,128)(2,1)S(1)}, u32[]{:S(2)}, u32[]{:S(2)}) %collective-permute-start) | collective-permute-done | bytes 344096 | tf_op jit(solution)/shard_map/ppermute | solution.py:318
  102.7 3.4 collective-permute-done.1
  106.8 3.4 copy-done
  110.2 3.0 attention.1.rows_ref.base_ref
  113.2 4.1 %send_rows.3 = bf16[3584,256]{1,0:T(8,128)(2,1)} custom-call(bf16[896,128]{1,0:T(8,128)(2,1)S(1)} %compare_convert_fusion.picker_ref, bf16[128,1024]{1,0:T(8,128)(2,1)S(1)} %attention.1.rows_ref.base_ref, bf16[4,448,112]{2,1,0:T(8,128)(2,1)S(1)} %copy-done.7), custom_call_target="tpu_custom_call" | custom-call | tf_op jit(solution)/shard_map/send_rows/pallas_call | solution.py:158
  117.2 20.6 %all-to-all-start.1 = ((bf16[64,56,256]{2,1,0:T(8,128)(2,1)}), bf16[64,56,256]{2,1,0:T(8,128)(2,1)}, u32[]{:S(2)}, u32[]{:S(2)}) async-start(bf16[64,56,256]{2,1,0:T(8,128)(2,1)} %bitcast.7), calls=%async_computation.1 | async-start | bytes 3670016 | tf_op jit(solution)/shard_map/all_to_all | solution.py:311
  137.8 2.5 copy.27
  140.3 43.1 %all-to-all-done.1 = bf16[64,56,256]{2,1,0:T(8,128)(2,1)} async-done(((bf16[64,56,256]{2,1,0:T(8,128)(2,1)}), bf16[64,56,256]{2,1,0:T(8,128)(2,1)}, u32[]{:S(2)}, u32[]{:S(2)}) %all-to-all-start.1) | async-done | bytes 1835040 | tf_op jit(solution)/shard_map/all_to_all | solution.py:311
  184.4 7.0 %first_product.3 = (bf16[896,1536]{1,0:T(8,128)(2,1)S(1)}, bf16[896,1024]{1,0:T(8,128)(2,1)S(1)}, bf16[896,128]{1,0:T(8,128)(2,1)S(1)}) custom-call(bf16[3584,256]{1,0:T(8,128)(2,1)} %bitcast.8.x_ref, bf16[4,112,448]{2,1,0:T(8,128)(2,1)S(1)} %copy-done.5, bf16[1024,1536]{1,0:T(8,128)(2,1)S(1)} %bitcast.25), custom_call_target="tpu_custom_call" | custom-call | tf_op jit(solution)/shard_map/first_product/pallas_call | solution.py:205
  191.6 1.1 copy-done.14
  192.9 1.2 collective-permute-start.3
  195.0 1.3 collective-permute-start.5
  196.3 16.3 %collective-permute-done.3 = bf16[224,1664]{1,0:T(8,128)(2,1)S(1)} collective-permute-done((bf16[224,1664]{1,0:T(8,128)(2,1)S(1)}, bf16[224,1664]{1,0:T(8,128)(2,1)S(1)}, u32[]{:S(2)}, u32[]{:S(2)}) %collective-permute-start.3) | collective-permute-done | bytes 745504 | tf_op jit(solution)/shard_map/ppermute | solution.py:318
  212.6 15.6 %collective-permute-done.4 = bf16[224,1664]{1,0:T(8,128)(2,1)S(1)} collective-permute-done((bf16[224,1664]{1,0:T(8,128)(2,1)S(1)}, bf16[224,1664]{1,0:T(8,128)(2,1)S(1)}, u32[]{:S(2)}, u32[]{:S(2)}) %collective-permute-start.4) | collective-permute-done | bytes 745504 | tf_op jit(solution)/shard_map/ppermute | solution.py:318
  228.8 2.9 add_reduce_fusion
  232.9 1.4 collective-permute-start.8
  234.4 1.2 convert_reduce_fusion
  235.8 2.0 pad_maximum_fusion.refs_0_
  237.8 7.3 %collective-permute-done.6.refs_1_ = bf16[224,768]{1,0:T(8,128)(2,1)} collective-permute-done((bf16[224,768]{1,0:T(8,128)(2,1)}, bf16[224,768]{1,0:T(8,128)(2,1)}, u32[]{:S(2)}, u32[]{:S(2)}) %collective-permute-start.6) | collective-permute-done | bytes 344096 | tf_op jit(solution)/shard_map/ppermute | solution.py:318
  245.2 3.7 collective-permute-done.8.refs_3_
  248.8 1.4 copy-done.11
  250.2 5.8 %second_product.2 = bf16[3584,256]{1,0:T(8,128)(2,1)S(1)} custom-call(s32[1]{0:T(128)} %bitcast.head_ref, bf16[224,768]{1,0:T(8,128)(2,1)} %get-tuple-element.25.refs_0_, bf16[224,768]{1,0:T(8,128)(2,1)} %collective-permute-done.6.refs_1_, bf16[224,768]{1,0:T(8,128)(2,1)} %collective-permute-done.7.refs_2_, bf16[224,768]{1,0:T(8,128)(2,1)} %collective-permute-done.8.refs_3_, ...), custom_call_target="tpu_custom_call" | custom-call | tf_op jit(solution)/shard_map/second_product/pallas_call | solution.py:279
  256.0 1.3 copy-done.3
  257.3 8.8 %all-to-all-start.2 = ((bf16[64,56,256]{2,1,0:T(8,128)(2,1)}), bf16[64,56,256]{2,1,0:T(8,128)(2,1)}, u32[]{:S(2)}, u32[]{:S(2)}) async-start(bf16[64,56,256]{2,1,0:T(8,128)(2,1)} %bitcast.31), calls=%async_computation.2 | async-start | bytes 3670016 | tf_op jit(solution)/shard_map/all_to_all | solution.py:311
  267.7 2.4 collective-permute-start.9
  270.1 17.3 %collective-permute-done.10.refs_2_ = bf16[224,1664]{1,0:T(8,128)(2,1)S(1)} collective-permute-done((bf16[224,1664]{1,0:T(8,128)(2,1)}, bf16[224,1664]{1,0:T(8,128)(2,1)S(1)}, u32[]{:S(2)}, u32[]{:S(2)}) %collective-permute-start.10) | collective-permute-done | bytes 745504 | tf_op jit(solution)/shard_map/ppermute | solution.py:318
  287.4 15.1 %collective-permute-done.11.refs_3_ = bf16[224,1664]{1,0:T(8,128)(2,1)S(1)} collective-permute-done((bf16[224,1664]{1,0:T(8,128)(2,1)}, bf16[224,1664]{1,0:T(8,128)(2,1)S(1)}, u32[]{:S(2)}, u32[]{:S(2)}) %collective-permute-start.11) | collective-permute-done | bytes 745504 | tf_op jit(solution)/shard_map/ppermute | solution.py:318
  302.6 1.0 copy-done.9
  303.6 1.1 copy-done.13
  304.7 1.5 copy-done.15
  306.2 6.2 %second_product.3 = bf16[3584,256]{1,0:T(8,128)(2,1)S(1)} custom-call(s32[1]{0:T(128)} %bitcast.head_ref, bf16[224,1664]{1,0:T(8,128)(2,1)S(1)} %copy-done.13, bf16[224,1664]{1,0:T(8,128)(2,1)S(1)} %collective-permute-done.9.refs_1_, bf16[224,1664]{1,0:T(8,128)(2,1)S(1)} %collective-permute-done.10.refs_2_, ...), custom_call_target="tpu_custom_call" | custom-call | tf_op jit(solution)/shard_map/second_product/pallas_call | solution.py:279
  312.5 1.2 copy-done.1
  313.7 10.4 %all-to-all-start.3 = ((bf16[64,56,256]{2,1,0:T(8,128)(2,1)}), bf16[64,56,256]{2,1,0:T(8,128)(2,1)S(1)}, u32[]{:S(2)}, u32[]{:S(2)}) async-start(bf16[64,56,256]{2,1,0:T(8,128)(2,1)} %bitcast.27), calls=%async_computation.3 | async-start | bytes 3670016 | tf_op jit(solution)/shard_map/all_to_all | solution.py:311
  324.2 4.0 %combine.2 = bf16[128,1024]{1,0:T(8,128)(2,1)} custom-call(bf16[3584,256]{1,0:T(8,128)(2,1)} %bitcast.11.came_ref, bf16[4,112,448]{2,1,0:T(8,128)(2,1)S(1)} %copy-done.6, bf16[256,896]{1,0:T(8,128)(2,1)S(1)} %copy-done.12, bf16[128,1024]{1,0:T(8,128)(2,1)S(1)} %attention.1.rows_ref.base_ref), custom_call_target="tpu_custom_call" | custom-call | tf_op jit(solution)/shard_map/combine/pallas_call | solution.py:301
  328.2 41.6 %all-to-all-done.3 = bf16[64,56,256]{2,1,0:T(8,128)(2,1)S(1)} async-done(((bf16[64,56,256]{2,1,0:T(8,128)(2,1)}), bf16[64,56,256]{2,1,0:T(8,128)(2,1)S(1)}, u32[]{:S(2)}, u32[]{:S(2)}) %all-to-all-start.3) | async-done | bytes 1835040 | tf_op jit(solution)/shard_map/all_to_all | solution.py:311
  369.8 2.5 combine.3
  (87 shorter events, 12.0 us)
Async XLA Ops:
  7.2 3.8 copy-start.7
  7.2 3.8 copy-start.16
  7.2 99.6 %all-gather.2.cloned.1.call-start = ((), (), s32[]{:S(2)}) async-start(), calls=%async_computation.4 | async-start | bytes 8519680 | tf_op jit(solution)/shard_map/all_gather | solution.py:364
  13.8 1.3 copy-start.2
  15.0 63.4 %all-to-all-start = ((bf16[64,56,256]{2,1,0:T(8,128)(2,1)}), bf16[64,56,256]{2,1,0:T(8,128)(2,1)S(1)}, u32[]{:S(2)}, u32[]{:S(2)}) async-start(bf16[64,56,256]{2,1,0:T(8,128)(2,1)} %bitcast.30), calls=%async_computation | async-start | bytes 3670016 | tf_op jit(solution)/shard_map/all_to_all | solution.py:311
  27.1 0.7 copy-start.27
  27.1 0.7 copy-start.28
  27.8 50.7 %copy-start.4 = (bf16[4,112,448]{2,1,0:T(8,128)(2,1)S(1)}, bf16[4,112,448]{2,1,0:T(8,128)(2,1)}, u32[]{:S(2)}) copy-start(bf16[4,112,448]{2,1,0:T(8,128)(2,1)} %constant.77.clone.gather_ref) | copy-start | bytes 1204228
  78.5 1.5 copy-start.10
  84.6 6.0 %copy-start.20 = (f32[128,896]{1,0:T(8,128)S(1)}, f32[128,896]{1,0:T(8,128)}, u32[]{:S(2)}) copy-start(f32[128,896]{1,0:T(8,128)} %copy.25) | copy-start | bytes 1376260
  84.6 6.0 %copy-start.22 = (bf16[128,896]{1,0:T(8,128)(2,1)S(1)}, bf16[128,896]{1,0:T(8,128)(2,1)}, u32[]{:S(2)}) copy-start(bf16[128,896]{1,0:T(8,128)(2,1)} %fusion.2) | copy-start | bytes 688132
  84.6 22.2 %copy-start.18 = (bf16[128,1024]{1,0:T(8,128)(2,1)S(1)}, bf16[128,1024]{1,0:T(8,128)(2,1)}, u32[]{:S(2)}) copy-start(bf16[128,1024]{1,0:T(8,128)(2,1)} %q_ref.1) | copy-start | bytes 786436
  85.5 17.2 %collective-permute-start = (bf16[224,768]{1,0:T(8,128)(2,1)S(1)}, bf16[224,768]{1,0:T(8,128)(2,1)S(1)}, u32[]{:S(2)}, u32[]{:S(2)}) collective-permute-start(bf16[224,768]{1,0:T(8,128)(2,1)S(1)} %get-tuple-element.43), channel_id=1, source_target_pairs={{1,0},{2,1},{3,2},{0,3},{5,4},{6,5},{7,6},{4,7},{9,8},{10,9},{11,1... | collective-permute-start | bytes 1032200 | tf_op jit(solution)/shard_map/ppermute | solution.py:318
  88.3 17.8 %collective-permute-start.1 = (bf16[224,768]{1,0:T(8,128)(2,1)S(1)}, bf16[224,768]{1,0:T(8,128)(2,1)S(1)}, u32[]{:S(2)}, u32[]{:S(2)}) collective-permute-start(bf16[224,768]{1,0:T(8,128)(2,1)S(1)} %get-tuple-element.42), channel_id=1, source_target_pairs={{3,0},{0,1},{1,2},{2,3},{7,4},{4,5},{5,6},{6,7},{11,8},{8,9},{9,10... | collective-permute-start | bytes 1032200 | tf_op jit(solution)/shard_map/ppermute | solution.py:318
  88.3 18.5 %collective-permute-start.2 = (bf16[224,768]{1,0:T(8,128)(2,1)S(1)}, bf16[224,768]{1,0:T(8,128)(2,1)}, u32[]{:S(2)}, u32[]{:S(2)}) collective-permute-start(bf16[224,768]{1,0:T(8,128)(2,1)S(1)} %get-tuple-element.41), channel_id=1, source_target_pairs={{2,0},{3,1},{0,2},{1,3},{6,4},{7,5},{4,6},{5,7},{10,8},{11,9},{8,1... | collective-permute-start | bytes 1032200 | tf_op jit(solution)/shard_map/ppermute | solution.py:318
  102.7 3.4 copy-start.23
  106.1 0.7 copy-start.25
  106.8 3.4 copy-start
  117.2 66.2 %all-to-all-start.1 = ((bf16[64,56,256]{2,1,0:T(8,128)(2,1)}), bf16[64,56,256]{2,1,0:T(8,128)(2,1)}, u32[]{:S(2)}, u32[]{:S(2)}) async-start(bf16[64,56,256]{2,1,0:T(8,128)(2,1)} %bitcast.7), calls=%async_computation.1 | async-start | bytes 3670016 | tf_op jit(solution)/shard_map/all_to_all | solution.py:311
  183.4 1.0 copy-start.5
  191.5 1.3 copy-start.14
  192.9 19.7 %collective-permute-start.3 = (bf16[224,1664]{1,0:T(8,128)(2,1)S(1)}, bf16[224,1664]{1,0:T(8,128)(2,1)S(1)}, u32[]{:S(2)}, u32[]{:S(2)}) collective-permute-start(bf16[224,1664]{1,0:T(8,128)(2,1)S(1)} %get-tuple-element.37), channel_id=1, source_target_pairs={{1,0},{2,1},{3,2},{0,3},{5,4},{6,5},{7,6},{4,7},{9,8},{10,9},{11,1... | collective-permute-start | bytes 2236424 | tf_op jit(solution)/shard_map/ppermute | solution.py:318
  194.2 34.0 %collective-permute-start.4 = (bf16[224,1664]{1,0:T(8,128)(2,1)S(1)}, bf16[224,1664]{1,0:T(8,128)(2,1)S(1)}, u32[]{:S(2)}, u32[]{:S(2)}) collective-permute-start(bf16[224,1664]{1,0:T(8,128)(2,1)S(1)} %get-tuple-element.39), channel_id=1, source_target_pairs={{3,0},{0,1},{1,2},{2,3},{7,4},{4,5},{5,6},{6,7},{11,8},{8,9},{9,10... | collective-permute-start | bytes 2236424 | tf_op jit(solution)/shard_map/ppermute | solution.py:318
  195.0 33.2 %collective-permute-start.5 = (bf16[224,1664]{1,0:T(8,128)(2,1)S(1)}, bf16[224,1664]{1,0:T(8,128)(2,1)S(1)}, u32[]{:S(2)}, u32[]{:S(2)}) collective-permute-start(bf16[224,1664]{1,0:T(8,128)(2,1)S(1)} %get-tuple-element.38), channel_id=1, source_target_pairs={{2,0},{3,1},{0,2},{1,3},{6,4},{7,5},{4,6},{5,7},{10,8},{11,9},{8,1... | collective-permute-start | bytes 2236424 | tf_op jit(solution)/shard_map/ppermute | solution.py:318
  196.3 32.5 %copy-start.21 = (bf16[224,768]{1,0:T(8,128)(2,1)S(1)}, bf16[224,768]{1,0:T(8,128)(2,1)}, u32[]{:S(2)}) copy-start(bf16[224,768]{1,0:T(8,128)(2,1)} %get-tuple-element.18) | copy-start | bytes 1032196
  196.3 32.5 %copy-start.24 = (bf16[224,768]{1,0:T(8,128)(2,1)S(1)}, bf16[224,768]{1,0:T(8,128)(2,1)}, u32[]{:S(2)}) copy-start(bf16[224,768]{1,0:T(8,128)(2,1)} %copy-done.23) | copy-start | bytes 1032196
  196.3 32.5 %copy-start.26 = (bf16[224,768]{1,0:T(8,128)(2,1)S(1)}, bf16[224,768]{1,0:T(8,128)(2,1)}, u32[]{:S(2)}) copy-start(bf16[224,768]{1,0:T(8,128)(2,1)} %copy-done.25) | copy-start | bytes 1032196
  228.6 3.1 copy-start.19
  231.7 13.5 %collective-permute-start.6 = (bf16[224,768]{1,0:T(8,128)(2,1)}, bf16[224,768]{1,0:T(8,128)(2,1)}, u32[]{:S(2)}, u32[]{:S(2)}) collective-permute-start(bf16[224,768]{1,0:T(8,128)(2,1)} %get-tuple-element.25.refs_0_), channel_id=1, source_target_pairs={{1,0},{2,1},{3,2},{0,3},{5,4},{6,5},{7,6},{4,7},{9,8},{10,9},{11,1... | collective-permute-start | bytes 1032200 | tf_op jit(solution)/shard_map/ppermute | solution.py:318
  232.3 12.8 %collective-permute-start.7 = (bf16[224,768]{1,0:T(8,128)(2,1)}, bf16[224,768]{1,0:T(8,128)(2,1)}, u32[]{:S(2)}, u32[]{:S(2)}) collective-permute-start(bf16[224,768]{1,0:T(8,128)(2,1)} %get-tuple-element.25.refs_0_), channel_id=1, source_target_pairs={{2,0},{3,1},{0,2},{1,3},{6,4},{7,5},{4,6},{5,7},{10,8},{11,9},{8,1... | collective-permute-start | bytes 1032200 | tf_op jit(solution)/shard_map/ppermute | solution.py:318
  232.9 15.9 %collective-permute-start.8 = (bf16[224,768]{1,0:T(8,128)(2,1)}, bf16[224,768]{1,0:T(8,128)(2,1)}, u32[]{:S(2)}, u32[]{:S(2)}) collective-permute-start(bf16[224,768]{1,0:T(8,128)(2,1)} %get-tuple-element.25.refs_0_), channel_id=1, source_target_pairs={{3,0},{0,1},{1,2},{2,3},{7,4},{4,5},{5,6},{6,7},{11,8},{8,9},{9,10... | collective-permute-start | bytes 1032200 | tf_op jit(solution)/shard_map/ppermute | solution.py:318
  234.4 14.4 %copy-start.8 = (bf16[4,448,112]{2,1,0:T(8,128)(2,1)S(1)}, bf16[4,448,112]{2,1,0:T(8,128)(2,1)}, u32[]{:S(2)}) copy-start(bf16[4,448,112]{2,1,0:T(8,128)(2,1)} %constant.76.clone.spread_ref.refs_5_) | copy-start | bytes 1204228
  248.8 1.4 copy-start.11
  256.0 1.3 copy-start.3
  257.3 56.4 %all-to-all-start.2 = ((bf16[64,56,256]{2,1,0:T(8,128)(2,1)}), bf16[64,56,256]{2,1,0:T(8,128)(2,1)}, u32[]{:S(2)}, u32[]{:S(2)}) async-start(bf16[64,56,256]{2,1,0:T(8,128)(2,1)} %bitcast.31), calls=%async_computation.2 | async-start | bytes 3670016 | tf_op jit(solution)/shard_map/all_to_all | solution.py:311
  266.1 21.4 %collective-permute-start.10 = (bf16[224,1664]{1,0:T(8,128)(2,1)}, bf16[224,1664]{1,0:T(8,128)(2,1)S(1)}, u32[]{:S(2)}, u32[]{:S(2)}) collective-permute-start(bf16[224,1664]{1,0:T(8,128)(2,1)} %pad_maximum_fusion.refs_0_), channel_id=1, source_target_pairs={{2,0},{3,1},{0,2},{1,3},{6,4},{7,5},{4,6},{5,7},{10,8},{11,9},{8,1... | collective-permute-start | bytes 2236424 | tf_op jit(solution)/shard_map/ppermute | solution.py:318
  266.9 35.7 %collective-permute-start.11 = (bf16[224,1664]{1,0:T(8,128)(2,1)}, bf16[224,1664]{1,0:T(8,128)(2,1)S(1)}, u32[]{:S(2)}, u32[]{:S(2)}) collective-permute-start(bf16[224,1664]{1,0:T(8,128)(2,1)} %pad_maximum_fusion.refs_0_), channel_id=1, source_target_pairs={{3,0},{0,1},{1,2},{2,3},{7,4},{4,5},{5,6},{6,7},{11,8},{8,9},{9,10... | collective-permute-start | bytes 2236424 | tf_op jit(solution)/shard_map/ppermute | solution.py:318
  267.7 34.9 %collective-permute-start.9 = (bf16[224,1664]{1,0:T(8,128)(2,1)}, bf16[224,1664]{1,0:T(8,128)(2,1)S(1)}, u32[]{:S(2)}, u32[]{:S(2)}) collective-permute-start(bf16[224,1664]{1,0:T(8,128)(2,1)} %pad_maximum_fusion.refs_0_), channel_id=1, source_target_pairs={{1,0},{2,1},{3,2},{0,3},{5,4},{6,5},{7,6},{4,7},{9,8},{10,9},{11,1... | collective-permute-start | bytes 2236424 | tf_op jit(solution)/shard_map/ppermute | solution.py:318
  302.6 1.0 copy-start.9
  303.6 1.1 copy-start.13
  304.7 1.5 copy-start.15
  312.4 1.3 copy-start.1
  313.7 10.5 %copy-start.6 = (bf16[4,112,448]{2,1,0:T(8,128)(2,1)S(1)}, bf16[4,112,448]{2,1,0:T(8,128)(2,1)}, u32[]{:S(2)}) copy-start(bf16[4,112,448]{2,1,0:T(8,128)(2,1)} %constant.77.clone.gather_ref) | copy-start | bytes 1204228
  313.7 10.5 %copy-start.12 = (bf16[256,896]{1,0:T(8,128)(2,1)S(1)}, bf16[256,896]{1,0:T(8,128)(2,1)}, u32[]{:S(2)}) copy-start(bf16[256,896]{1,0:T(8,128)(2,1)} %pad_maximum_fusion.1.weight_ref) | copy-start | bytes 1376260
  313.7 56.1 %all-to-all-start.3 = ((bf16[64,56,256]{2,1,0:T(8,128)(2,1)}), bf16[64,56,256]{2,1,0:T(8,128)(2,1)S(1)}, u32[]{:S(2)}, u32[]{:S(2)}) async-start(bf16[64,56,256]{2,1,0:T(8,128)(2,1)} %bitcast.27), calls=%async_computation.3 | async-start | bytes 3670016 | tf_op jit(solution)/shard_map/all_to_all | solution.py:311
  324.2 45.6 %copy-start.17 = (bf16[128,1024]{1,0:T(8,128)(2,1)S(1)}, bf16[128,1024]{1,0:T(8,128)(2,1)}, u32[]{:S(2)}) copy-start(bf16[128,1024]{1,0:T(8,128)(2,1)} %base_ref.1) | copy-start | bytes 786436
Sparse Core Ops, SparseCore 0:
  10.8 92.2 all-gather.1

commit v3 on v2

--- a/solution.py
+++ b/solution.py
@@ -138,7 +138,7 @@
             ],
         ),
         out_shape=jax.ShapeDtypeStruct((ROWS, WIDTH), BF16),
-        compiler_params=params(40),
+        compiler_params=params(58),
         name="attention",
     )(place, queries, kv)
 
@@ -335,6 +335,14 @@
     return [x] + [parts[d] for d in range(1, HEAD_COUNT)]
 
 
+def head_gather_twice(x):
+    half = x.shape[0] // 2
+    low = from_head(x, 3)
+    high = from_head(x, 1)
+    opposite = jnp.concatenate([from_head(low[:half], 3), from_head(high[half:], 1)])
+    return [x, high, opposite, low]
+
+
 def total(parts):
     return functools.reduce(jnp.add, [part.astype(F32) for part in parts])
 
@@ -347,6 +355,10 @@
     matrix = spread_matrix()
     spread = jnp.asarray(matrix, BF16)
     gather = jnp.asarray(matrix.transpose(0, 2, 1), BF16)
+
+    own_kv = jnp.concatenate([keys, values], axis=1)
+    own_kv, routes, route_weights = lax.optimization_barrier((own_kv, routes, route_weights))
+    kv = lax.all_gather(own_kv, "exp", axis=0, tiled=True)
 
     hits = routes[:, :, None] == jnp.arange(EXPERTS, dtype=jnp.int32)
     hit = jnp.any(hits, axis=1)
@@ -361,7 +373,6 @@
     weight_low = (weight - weight_high.astype(F32)).astype(BF16)
     weight_both = jnp.concatenate([weight_high, weight_low], axis=0)
 
-    kv = lax.all_gather(jnp.concatenate([keys, values], axis=1), "exp", axis=0, tiled=True)
     grads_in = exchange(send_rows(picker, grad_out, spread))
     back, _, _ = first_product(grads_in, gather, w_second, True)
     back = head_scatter(head, back)
@@ -390,7 +401,7 @@
     grad_hidden = jnp.concatenate([grad_gate, grad_up, correction], axis=1)
     grad_hidden, *gathered = lax.optimization_barrier((grad_hidden, *gathered))
     came_out = exchange(second_product(head, gathered, w_second, spread, False))
-    grad_hidden = head_gather(grad_hidden)
+    grad_hidden = head_gather_twice(grad_hidden)
     came_grad = exchange(second_product(head, grad_hidden, w_first, spread, True, rows))
     output = combine(came_out, gather, weight_both, attended)
     grad_attended = combine(came_grad, gather, weight_both, grad_out)

time: 380 us -> 373 us (0.982)
  local copies, waits for them, and re-layouts: 25.9 us -> 22 us
    ppermute x12 -> x13, waiting for transfers between devices: 90 us -> 81.4 us  [from_head(): lax.ppermute(x, 'head', [((i + d) % HEAD_COUNT, i) for i in range(HEAD_CO...]
    all_to_all x4, waiting for transfers between devices: 129 us -> 134 us  [exchange(): lax.all_to_all(x.reshape(EXPERTS, CAP * PIECES, PIECE), 'exp', split_axis...]
    all_to_all x4, starting transfers between devices: 51.8 us -> 47.2 us  [exchange(): lax.all_to_all(x.reshape(EXPERTS, CAP * PIECES, PIECE), 'exp', split_axis...]
    unnamed x60, local copies, waits for them, and re-layouts: 19.5 us -> 14.9 us
    ppermute x12 -> x13, starting transfers between devices: 15.1 us -> 17.5 us  [from_head(): lax.ppermute(x, 'head', [((i + d) % HEAD_COUNT, i) for i in range(HEAD_CO...]
  transfers between devices with their start and end apart: 17 -> 18, of which waited for: 11 -> 13; matrix products, arithmetic and copies ran while one was open for 4% -> 5% of each run, Pallas kernels for 5% -> 5%
where the time goes in v3:
time: 373 us; the launch traced here: 372 us
  waiting for transfers between devices  216 us (58%)
  starting transfers between devices  64.7 us (17%)
  Pallas kernels  41.9 us (11%)
  local copies, waits for them, and re-layouts  22 us (6%)
  between operations  14.6 us (4%)
  other arithmetic  12 us (3%)
    all_to_all x4, waiting for transfers between devices, exchange(): lax.all_to_all(x.reshape(EXPERTS, CAP * PIECES, PIECE), 'exp', split_axis...  134 us
    ppermute x13, waiting for transfers between devices, from_head(): lax.ppermute(x, 'head', [((i + d) % HEAD_COUNT, i) for i in range(HEAD_CO...  81.4 us
    all_to_all x4, starting transfers between devices, exchange(): lax.all_to_all(x.reshape(EXPERTS, CAP * PIECES, PIECE), 'exp', split_axis...  47.2 us
    ppermute x13, starting transfers between devices, from_head(): lax.ppermute(x, 'head', [((i + d) % HEAD_COUNT, i) for i in range(HEAD_CO...  17.5 us
    unnamed x60, local copies, waits for them, and re-layouts  14.9 us
    pallas_call x2, Pallas kernels, second_product(): pl.pallas_call(functools.partial(second_kernel, by_rows, rows is not None...  11.9 us
    pallas_call x2, Pallas kernels, first_product(): pl.pallas_call(functools.partial(first_kernel, by_rows), grid=(outs // TI...  11.7 us
  transfers between devices with their start and end apart: 18, of which 13 were waited for; matrix products, arithmetic and copies ran while one was open for 5% of the time, Pallas kernels for 5%

profile of v3, /device:TPU:2, one launch (start us, length us, event | category | flops | bytes accessed | tf_op | source)
XLA Modules:
  0.0 371.6 jit_solution(9203269191931017961)
XLA Ops:
  7.2 1.6 pad_maximum_fusion.3
  10.9 2.8 send_rows.2
  13.8 1.3 copy-done.1
  15.0 12.0 %all-to-all-start = ((bf16[64,56,256]{2,1,0:T(8,128)(2,1)}), bf16[64,56,256]{2,1,0:T(8,128)(2,1)S(1)}, u32[]{:S(2)}, u32[]{:S(2)}) async-start(bf16[64,56,256]{2,1,0:T(8,128)(2,1)} %bitcast.30), calls=%async_computation | async-start | bytes 3670016 | tf_op jit(solution)/shard_map/all_to_all | solution.py:311
  28.6 1.9 broadcast_in_dim.79
  30.5 2.0 copy.25
  32.5 1.8 fusion.2
  34.2 44.5 %all-to-all-done = bf16[64,56,256]{2,1,0:T(8,128)(2,1)S(1)} async-done(((bf16[64,56,256]{2,1,0:T(8,128)(2,1)}), bf16[64,56,256]{2,1,0:T(8,128)(2,1)S(1)}, u32[]{:S(2)}, u32[]{:S(2)}) %all-to-all-start) | async-done | bytes 1835040 | tf_op jit(solution)/shard_map/all_to_all | solution.py:311
  78.7 1.4 copy-done.9
  80.1 4.7 %first_product.2 = (bf16[896,768]{1,0:T(8,128)(2,1)S(1)}, bf16[896,1024]{1,0:T(8,128)(2,1)}, bf16[896,128]{1,0:T(8,128)(2,1)}) custom-call(bf16[3584,256]{1,0:T(8,128)(2,1)S(1)} %bitcast.29, bf16[4,112,448]{2,1,0:T(8,128)(2,1)S(1)} %copy-done.3, bf16[768,1024]{1,0:T(8,128)(2,1)S(1)} %bitcast.32), custom_call_target="tpu_custom_call" | custom-call | tf_op jit(solution)/shard_map/first_product/pallas_call | solution.py:205
  85.7 2.7 collective-permute-start
  88.4 2.3 collective-permute-start.2
  91.6 11.1 %collective-permute-done = bf16[224,768]{1,0:T(8,128)(2,1)S(1)} collective-permute-done((bf16[224,768]{1,0:T(8,128)(2,1)S(1)}, bf16[224,768]{1,0:T(8,128)(2,1)S(1)}, u32[]{:S(2)}, u32[]{:S(2)}) %collective-permute-start) | collective-permute-done | bytes 344096 | tf_op jit(solution)/shard_map/ppermute | solution.py:318
  102.8 3.4 collective-permute-done.1
  106.9 5.0 %attention.1.rows_ref.base_ref = bf16[128,1024]{1,0:T(8,128)(2,1)} custom-call(s32[1]{0:T(128)} %bitcast.6.place_ref, bf16[128,1024]{1,0:T(8,128)(2,1)} %q_ref.1, bf16[8192,512]{1,0:T(8,128)(2,1)} %all-gather.2.cloned.1.call-done.kv_ref), custom_call_target="tpu_custom_call" | custom-call | tf_op jit(solution)/shard_map/attention/pallas_call | solution.py:123
  112.8 4.1 %send_rows.3 = bf16[3584,256]{1,0:T(8,128)(2,1)} custom-call(bf16[896,128]{1,0:T(8,128)(2,1)S(1)} %compare_convert_fusion.picker_ref, bf16[128,1024]{1,0:T(8,128)(2,1)S(1)} %copy-done.13, bf16[4,448,112]{2,1,0:T(8,128)(2,1)S(1)} %copy-done.6), custom_call_target="tpu_custom_call" | custom-call | tf_op jit(solution)/shard_map/send_rows/pallas_call | solution.py:158
  116.9 20.8 %all-to-all-start.1 = ((bf16[64,56,256]{2,1,0:T(8,128)(2,1)}), bf16[64,56,256]{2,1,0:T(8,128)(2,1)}, u32[]{:S(2)}, u32[]{:S(2)}) async-start(bf16[64,56,256]{2,1,0:T(8,128)(2,1)} %bitcast.7), calls=%async_computation.1 | async-start | bytes 3670016 | tf_op jit(solution)/shard_map/all_to_all | solution.py:311
  137.7 2.5 copy.27
  140.1 43.1 %all-to-all-done.1 = bf16[64,56,256]{2,1,0:T(8,128)(2,1)} async-done(((bf16[64,56,256]{2,1,0:T(8,128)(2,1)}), bf16[64,56,256]{2,1,0:T(8,128)(2,1)}, u32[]{:S(2)}, u32[]{:S(2)}) %all-to-all-start.1) | async-done | bytes 1835040 | tf_op jit(solution)/shard_map/all_to_all | solution.py:311
  183.2 1.0 copy-done.4
  184.3 7.0 %first_product.3 = (bf16[896,1536]{1,0:T(8,128)(2,1)S(1)}, bf16[896,1024]{1,0:T(8,128)(2,1)S(1)}, bf16[896,128]{1,0:T(8,128)(2,1)S(1)}) custom-call(bf16[3584,256]{1,0:T(8,128)(2,1)} %bitcast.8.x_ref, bf16[4,112,448]{2,1,0:T(8,128)(2,1)S(1)} %copy-done.4, bf16[1024,1536]{1,0:T(8,128)(2,1)S(1)} %bitcast.25), custom_call_target="tpu_custom_call" | custom-call | tf_op jit(solution)/shard_map/first_product/pallas_call | solution.py:205
  191.5 1.1 copy-done.15
  192.8 1.1 collective-permute-start.3
  193.9 1.0 collective-permute-start.4
  195.8 16.6 %collective-permute-done.3 = bf16[224,1664]{1,0:T(8,128)(2,1)S(1)} collective-permute-done((bf16[224,1664]{1,0:T(8,128)(2,1)S(1)}, bf16[224,1664]{1,0:T(8,128)(2,1)S(1)}, u32[]{:S(2)}, u32[]{:S(2)}) %collective-permute-start.3) | collective-permute-done | bytes 745504 | tf_op jit(solution)/shard_map/ppermute | solution.py:318
  212.5 15.4 %collective-permute-done.4 = bf16[224,1664]{1,0:T(8,128)(2,1)S(1)} collective-permute-done((bf16[224,1664]{1,0:T(8,128)(2,1)S(1)}, bf16[224,1664]{1,0:T(8,128)(2,1)S(1)}, u32[]{:S(2)}, u32[]{:S(2)}) %collective-permute-start.4) | collective-permute-done | bytes 745504 | tf_op jit(solution)/shard_map/ppermute | solution.py:318
  228.5 2.8 add_reduce_fusion
  232.7 1.3 collective-permute-start.8
  234.8 1.3 convert_reduce_fusion
  236.2 2.0 pad_maximum_fusion.refs_0_
  238.2 6.3 %collective-permute-done.6.refs_1_ = bf16[224,768]{1,0:T(8,128)(2,1)} collective-permute-done((bf16[224,768]{1,0:T(8,128)(2,1)S(1)}, bf16[224,768]{1,0:T(8,128)(2,1)}, u32[]{:S(2)}, u32[]{:S(2)}) %collective-permute-start.6) | collective-permute-done | bytes 344096 | tf_op jit(solution)/shard_map/ppermute | solution.py:318
  244.7 3.7 collective-permute-done.8.refs_3_
  248.3 1.4 copy-done.10
  249.8 5.7 %second_product.2 = bf16[3584,256]{1,0:T(8,128)(2,1)S(1)} custom-call(s32[1]{0:T(128)} %bitcast.head_ref, bf16[224,768]{1,0:T(8,128)(2,1)S(1)} %get-tuple-element.31.refs_0_, bf16[224,768]{1,0:T(8,128)(2,1)} %collective-permute-done.6.refs_1_, bf16[224,768]{1,0:T(8,128)(2,1)} %collective-permute-done.7.refs_2_, ...), custom_call_target="tpu_custom_call" | custom-call | tf_op jit(solution)/shard_map/second_product/pallas_call | solution.py:279
  255.4 1.3 copy-done.2
  256.7 8.8 %all-to-all-start.2 = ((bf16[64,56,256]{2,1,0:T(8,128)(2,1)}), bf16[64,56,256]{2,1,0:T(8,128)(2,1)}, u32[]{:S(2)}, u32[]{:S(2)}) async-start(bf16[64,56,256]{2,1,0:T(8,128)(2,1)} %bitcast.31), calls=%async_computation.2 | async-start | bytes 3670016 | tf_op jit(solution)/shard_map/all_to_all | solution.py:311
  265.6 3.2 collective-permute-start.9
  268.8 16.9 %collective-permute-done.10.refs_3_ = bf16[224,1664]{1,0:T(8,128)(2,1)S(1)} collective-permute-done((bf16[224,1664]{1,0:T(8,128)(2,1)}, bf16[224,1664]{1,0:T(8,128)(2,1)S(1)}, u32[]{:S(2)}, u32[]{:S(2)}) %collective-permute-start.10) | collective-permute-done | bytes 745504 | tf_op jit(solution)/shard_map/ppermute | solution.py:318
  285.9 3.3 collective-permute-start.12
  289.2 7.9 %collective-permute-done.11 = bf16[112,1664]{1,0:T(8,128)(2,1)S(1)} collective-permute-done((bf16[112,1664]{1,0:T(8,128)(2,1)S(1)}, bf16[112,1664]{1,0:T(8,128)(2,1)S(1)}, u32[]{:S(2)}, u32[]{:S(2)}) %collective-permute-start.11) | collective-permute-done | bytes 372768 | tf_op jit(solution)/shard_map/ppermute | solution.py:318
  297.2 1.5 copy-done.16
  298.6 6.2 %second_product.3 = bf16[3584,256]{1,0:T(8,128)(2,1)S(1)} custom-call(s32[1]{0:T(128)} %bitcast.head_ref, bf16[224,1664]{1,0:T(8,128)(2,1)S(1)} %copy-done.12, bf16[224,1664]{1,0:T(8,128)(2,1)S(1)} %collective-permute-done.9.refs_1_, bf16[224,1664]{1,0:T(8,128)(2,1)S(1)} %pad_maximum_fusion.1.refs_2_, bf16[224,1664]{1,0:T(8,128)(2,1)S(1)} %collective-permute-done.10.refs_3_, ...), custom_call_target="tpu_custom_call" | custom-call | tf_op jit(solution)/shard_map/second_product/pallas_call | solution.py:279
  304.9 1.2 copy-done
  306.1 5.0 %all-to-all-done.2 = bf16[64,56,256]{2,1,0:T(8,128)(2,1)} async-done(((bf16[64,56,256]{2,1,0:T(8,128)(2,1)}), bf16[64,56,256]{2,1,0:T(8,128)(2,1)}, u32[]{:S(2)}, u32[]{:S(2)}) %all-to-all-start.2) | async-done | bytes 1835040 | tf_op jit(solution)/shard_map/all_to_all | solution.py:311
  311.1 5.6 %all-to-all-start.3 = ((bf16[64,56,256]{2,1,0:T(8,128)(2,1)}), bf16[64,56,256]{2,1,0:T(8,128)(2,1)S(1)}, u32[]{:S(2)}, u32[]{:S(2)}) async-start(bf16[64,56,256]{2,1,0:T(8,128)(2,1)} %bitcast.27), calls=%async_computation.3 | async-start | bytes 3670016 | tf_op jit(solution)/shard_map/all_to_all | solution.py:311
  316.7 4.0 %combine.2 = bf16[128,1024]{1,0:T(8,128)(2,1)} custom-call(bf16[3584,256]{1,0:T(8,128)(2,1)} %bitcast.11.came_ref, bf16[4,112,448]{2,1,0:T(8,128)(2,1)S(1)} %copy-done.5, bf16[256,896]{1,0:T(8,128)(2,1)S(1)} %copy-done.11, bf16[128,1024]{1,0:T(8,128)(2,1)S(1)} %copy-done.14), custom_call_target="tpu_custom_call" | custom-call | tf_op jit(solution)/shard_map/combine/pallas_call | solution.py:301
  320.7 41.6 %all-to-all-done.3 = bf16[64,56,256]{2,1,0:T(8,128)(2,1)S(1)} async-done(((bf16[64,56,256]{2,1,0:T(8,128)(2,1)}), bf16[64,56,256]{2,1,0:T(8,128)(2,1)S(1)}, u32[]{:S(2)}, u32[]{:S(2)}) %all-to-all-start.3) | async-done | bytes 1835040 | tf_op jit(solution)/shard_map/all_to_all | solution.py:311
  362.3 2.5 combine.3
  (92 shorter events, 11.6 us)
Async XLA Ops:
  7.2 3.7 %copy-start.6 = (bf16[4,448,112]{2,1,0:T(8,128)(2,1)S(1)}, bf16[4,448,112]{2,1,0:T(8,128)(2,1)}, u32[]{:S(2)}) copy-start(bf16[4,448,112]{2,1,0:T(8,128)(2,1)} %constant.76.clone.spread_ref.refs_5_) | copy-start | bytes 1204228
  7.2 3.7 %copy-start.17 = (bf16[128,1024]{1,0:T(8,128)(2,1)S(1)}, bf16[128,1024]{1,0:T(8,128)(2,1)}, u32[]{:S(2)}) copy-start(bf16[128,1024]{1,0:T(8,128)(2,1)} %base_ref.1) | copy-start | bytes 786436
  7.2 99.7 %all-gather.2.cloned.1.call-start = ((), (), s32[]{:S(2)}) async-start(), calls=%async_computation.4 | async-start | bytes 8519680 | tf_op jit(solution)/shard_map/all_gather | solution.py:361
  13.8 1.3 copy-start.1
  15.0 63.7 %all-to-all-start = ((bf16[64,56,256]{2,1,0:T(8,128)(2,1)}), bf16[64,56,256]{2,1,0:T(8,128)(2,1)S(1)}, u32[]{:S(2)}, u32[]{:S(2)}) async-start(bf16[64,56,256]{2,1,0:T(8,128)(2,1)} %bitcast.30), calls=%async_computation | async-start | bytes 3670016 | tf_op jit(solution)/shard_map/all_to_all | solution.py:311
  27.0 0.7 copy-start.27
  27.1 0.7 copy-start.28
  27.7 50.9 %copy-start.3 = (bf16[4,112,448]{2,1,0:T(8,128)(2,1)S(1)}, bf16[4,112,448]{2,1,0:T(8,128)(2,1)}, u32[]{:S(2)}) copy-start(bf16[4,112,448]{2,1,0:T(8,128)(2,1)} %constant.77.clone.gather_ref) | copy-start | bytes 1204228
  78.7 1.5 copy-start.9
  84.8 5.9 %copy-start.20 = (f32[128,896]{1,0:T(8,128)S(1)}, f32[128,896]{1,0:T(8,128)}, u32[]{:S(2)}) copy-start(f32[128,896]{1,0:T(8,128)} %copy.25) | copy-start | bytes 1376260
  84.8 6.0 %copy-start.22 = (bf16[128,896]{1,0:T(8,128)(2,1)S(1)}, bf16[128,896]{1,0:T(8,128)(2,1)}, u32[]{:S(2)}) copy-start(bf16[128,896]{1,0:T(8,128)(2,1)} %fusion.2) | copy-start | bytes 688132
  85.7 17.1 %collective-permute-start = (bf16[224,768]{1,0:T(8,128)(2,1)S(1)}, bf16[224,768]{1,0:T(8,128)(2,1)S(1)}, u32[]{:S(2)}, u32[]{:S(2)}) collective-permute-start(bf16[224,768]{1,0:T(8,128)(2,1)S(1)} %get-tuple-element.49), channel_id=1, source_target_pairs={{1,0},{2,1},{3,2},{0,3},{5,4},{6,5},{7,6},{4,7},{9,8},{10,9},{11,1... | collective-permute-start | bytes 1032200 | tf_op jit(solution)/shard_map/ppermute | solution.py:318
  88.4 17.7 %collective-permute-start.1 = (bf16[224,768]{1,0:T(8,128)(2,1)S(1)}, bf16[224,768]{1,0:T(8,128)(2,1)S(1)}, u32[]{:S(2)}, u32[]{:S(2)}) collective-permute-start(bf16[224,768]{1,0:T(8,128)(2,1)S(1)} %get-tuple-element.48), channel_id=1, source_target_pairs={{3,0},{0,1},{1,2},{2,3},{7,4},{4,5},{5,6},{6,7},{11,8},{8,9},{9,10... | collective-permute-start | bytes 1032200 | tf_op jit(solution)/shard_map/ppermute | solution.py:318
  88.4 18.5 %collective-permute-start.2 = (bf16[224,768]{1,0:T(8,128)(2,1)S(1)}, bf16[224,768]{1,0:T(8,128)(2,1)}, u32[]{:S(2)}, u32[]{:S(2)}) collective-permute-start(bf16[224,768]{1,0:T(8,128)(2,1)S(1)} %get-tuple-element.47), channel_id=1, source_target_pairs={{2,0},{3,1},{0,2},{1,3},{6,4},{7,5},{4,6},{5,7},{10,8},{11,9},{8,1... | collective-permute-start | bytes 1032200 | tf_op jit(solution)/shard_map/ppermute | solution.py:318
  102.8 3.4 copy-start.23
  106.1 0.7 copy-start.25
  111.9 0.9 copy-start.13
  116.9 66.4 %all-to-all-start.1 = ((bf16[64,56,256]{2,1,0:T(8,128)(2,1)}), bf16[64,56,256]{2,1,0:T(8,128)(2,1)}, u32[]{:S(2)}, u32[]{:S(2)}) async-start(bf16[64,56,256]{2,1,0:T(8,128)(2,1)} %bitcast.7), calls=%async_computation.1 | async-start | bytes 3670016 | tf_op jit(solution)/shard_map/all_to_all | solution.py:311
  183.2 1.0 copy-start.4
  191.3 1.3 copy-start.15
  192.8 19.7 %collective-permute-start.3 = (bf16[224,1664]{1,0:T(8,128)(2,1)S(1)}, bf16[224,1664]{1,0:T(8,128)(2,1)S(1)}, u32[]{:S(2)}, u32[]{:S(2)}) collective-permute-start(bf16[224,1664]{1,0:T(8,128)(2,1)S(1)} %get-tuple-element.43), channel_id=1, source_target_pairs={{1,0},{2,1},{3,2},{0,3},{5,4},{6,5},{7,6},{4,7},{9,8},{10,9},{11,1... | collective-permute-start | bytes 2236424 | tf_op jit(solution)/shard_map/ppermute | solution.py:318
  193.9 34.0 %collective-permute-start.4 = (bf16[224,1664]{1,0:T(8,128)(2,1)S(1)}, bf16[224,1664]{1,0:T(8,128)(2,1)S(1)}, u32[]{:S(2)}, u32[]{:S(2)}) collective-permute-start(bf16[224,1664]{1,0:T(8,128)(2,1)S(1)} %get-tuple-element.45), channel_id=1, source_target_pairs={{3,0},{0,1},{1,2},{2,3},{7,4},{4,5},{5,6},{6,7},{11,8},{8,9},{9,10... | collective-permute-start | bytes 2236424 | tf_op jit(solution)/shard_map/ppermute | solution.py:318
  194.9 33.0 %collective-permute-start.5 = (bf16[224,1664]{1,0:T(8,128)(2,1)S(1)}, bf16[224,1664]{1,0:T(8,128)(2,1)S(1)}, u32[]{:S(2)}, u32[]{:S(2)}) collective-permute-start(bf16[224,1664]{1,0:T(8,128)(2,1)S(1)} %get-tuple-element.44), channel_id=1, source_target_pairs={{2,0},{3,1},{0,2},{1,3},{6,4},{7,5},{4,6},{5,7},{10,8},{11,9},{8,1... | collective-permute-start | bytes 2236424 | tf_op jit(solution)/shard_map/ppermute | solution.py:318
  195.8 32.6 %copy-start.21 = (bf16[224,768]{1,0:T(8,128)(2,1)S(1)}, bf16[224,768]{1,0:T(8,128)(2,1)}, u32[]{:S(2)}) copy-start(bf16[224,768]{1,0:T(8,128)(2,1)} %get-tuple-element.24) | copy-start | bytes 1032196
  195.8 32.6 %copy-start.24 = (bf16[224,768]{1,0:T(8,128)(2,1)S(1)}, bf16[224,768]{1,0:T(8,128)(2,1)}, u32[]{:S(2)}) copy-start(bf16[224,768]{1,0:T(8,128)(2,1)} %copy-done.23) | copy-start | bytes 1032196
  195.8 32.6 %copy-start.26 = (bf16[224,768]{1,0:T(8,128)(2,1)S(1)}, bf16[224,768]{1,0:T(8,128)(2,1)}, u32[]{:S(2)}) copy-start(bf16[224,768]{1,0:T(8,128)(2,1)} %copy-done.25) | copy-start | bytes 1032196
  228.3 3.0 copy-start.19
  231.3 13.3 %collective-permute-start.6 = (bf16[224,768]{1,0:T(8,128)(2,1)S(1)}, bf16[224,768]{1,0:T(8,128)(2,1)}, u32[]{:S(2)}, u32[]{:S(2)}) collective-permute-start(bf16[224,768]{1,0:T(8,128)(2,1)S(1)} %get-tuple-element.31.refs_0_), channel_id=1, source_target_pairs={{1,0},{2,1},{3,2},{0,3},{5,4},{6,5},{7,6},{4,7},{9,8},{10,9},{11,1... | collective-permute-start | bytes 1032200 | tf_op jit(solution)/shard_map/ppermute | solution.py:318
  232.0 12.6 %collective-permute-start.7 = (bf16[224,768]{1,0:T(8,128)(2,1)S(1)}, bf16[224,768]{1,0:T(8,128)(2,1)}, u32[]{:S(2)}, u32[]{:S(2)}) collective-permute-start(bf16[224,768]{1,0:T(8,128)(2,1)S(1)} %get-tuple-element.31.refs_0_), channel_id=1, source_target_pairs={{2,0},{3,1},{0,2},{1,3},{6,4},{7,5},{4,6},{5,7},{10,8},{11,9},{8,1... | collective-permute-start | bytes 1032200 | tf_op jit(solution)/shard_map/ppermute | solution.py:318
  232.7 15.7 %collective-permute-start.8 = (bf16[224,768]{1,0:T(8,128)(2,1)S(1)}, bf16[224,768]{1,0:T(8,128)(2,1)}, u32[]{:S(2)}, u32[]{:S(2)}) collective-permute-start(bf16[224,768]{1,0:T(8,128)(2,1)S(1)} %get-tuple-element.31.refs_0_), channel_id=1, source_target_pairs={{3,0},{0,1},{1,2},{2,3},{7,4},{4,5},{5,6},{6,7},{11,8},{8,9},{9,10... | collective-permute-start | bytes 1032200 | tf_op jit(solution)/shard_map/ppermute | solution.py:318
  234.8 13.6 %copy-start.7 = (bf16[4,448,112]{2,1,0:T(8,128)(2,1)S(1)}, bf16[4,448,112]{2,1,0:T(8,128)(2,1)}, u32[]{:S(2)}) copy-start(bf16[4,448,112]{2,1,0:T(8,128)(2,1)} %constant.76.clone.spread_ref.refs_5_) | copy-start | bytes 1204228
  248.3 1.4 copy-start.10
  255.4 1.3 copy-start.2
  256.7 54.4 %all-to-all-start.2 = ((bf16[64,56,256]{2,1,0:T(8,128)(2,1)}), bf16[64,56,256]{2,1,0:T(8,128)(2,1)}, u32[]{:S(2)}, u32[]{:S(2)}) async-start(bf16[64,56,256]{2,1,0:T(8,128)(2,1)} %bitcast.31), calls=%async_computation.2 | async-start | bytes 3670016 | tf_op jit(solution)/shard_map/all_to_all | solution.py:311
  265.5 31.6 %copy-start.8 = (bf16[4,448,112]{2,1,0:T(8,128)(2,1)S(1)}, bf16[4,448,112]{2,1,0:T(8,128)(2,1)}, u32[]{:S(2)}) copy-start(bf16[4,448,112]{2,1,0:T(8,128)(2,1)} %constant.76.clone.spread_ref.refs_5_) | copy-start | bytes 1204228
  265.5 31.6 %copy-start.12 = (bf16[224,1664]{1,0:T(8,128)(2,1)S(1)}, bf16[224,1664]{1,0:T(8,128)(2,1)}, u32[]{:S(2)}) copy-start(bf16[224,1664]{1,0:T(8,128)(2,1)} %pad_maximum_fusion.refs_0_) | copy-start | bytes 2236420
  265.5 20.2 %collective-permute-start.10 = (bf16[224,1664]{1,0:T(8,128)(2,1)}, bf16[224,1664]{1,0:T(8,128)(2,1)S(1)}, u32[]{:S(2)}, u32[]{:S(2)}) collective-permute-start(bf16[224,1664]{1,0:T(8,128)(2,1)} %pad_maximum_fusion.refs_0_), channel_id=1, source_target_pairs={{3,0},{0,1},{1,2},{2,3},{7,4},{4,5},{5,6},{6,7},{11,8},{8,9},{9,10... | collective-permute-start | bytes 2236424 | tf_op jit(solution)/shard_map/ppermute | solution.py:318
  265.6 20.3 %collective-permute-start.9 = (bf16[224,1664]{1,0:T(8,128)(2,1)}, bf16[224,1664]{1,0:T(8,128)(2,1)S(1)}, u32[]{:S(2)}, u32[]{:S(2)}) collective-permute-start(bf16[224,1664]{1,0:T(8,128)(2,1)} %pad_maximum_fusion.refs_0_), channel_id=1, source_target_pairs={{1,0},{2,1},{3,2},{0,3},{5,4},{6,5},{7,6},{4,7},{9,8},{10,9},{11,1... | collective-permute-start | bytes 2236424 | tf_op jit(solution)/shard_map/ppermute | solution.py:318
  285.8 11.3 %collective-permute-start.11 = (bf16[112,1664]{1,0:T(8,128)(2,1)S(1)}, bf16[112,1664]{1,0:T(8,128)(2,1)S(1)}, u32[]{:S(2)}, u32[]{:S(2)}) collective-permute-start(bf16[112,1664]{1,0:T(8,128)(2,1)S(1)} %slice.28), channel_id=1, source_target_pairs={{3,0},{0,1},{1,2},{2,3},{7,4},{4,5},{5,6},{6,7},{11,8},{8,9},{9,10... | collective-permute-start | bytes 1118216 | tf_op jit(solution)/shard_map/ppermute | solution.py:318
  285.9 11.2 %collective-permute-start.12 = (bf16[112,1664]{1,0:T(8,128)(2,1)S(1)}, bf16[112,1664]{1,0:T(8,128)(2,1)S(1)}, u32[]{:S(2)}, u32[]{:S(2)}) collective-permute-start(bf16[112,1664]{1,0:T(8,128)(2,1)S(1)} %slice.29), channel_id=1, source_target_pairs={{1,0},{2,1},{3,2},{0,3},{5,4},{6,5},{7,6},{4,7},{9,8},{10,9},{11,1... | collective-permute-start | bytes 1118216 | tf_op jit(solution)/shard_map/ppermute | solution.py:318
  297.1 1.5 copy-start.16
  304.9 1.3 copy-start
  311.1 5.6 %copy-start.5 = (bf16[4,112,448]{2,1,0:T(8,128)(2,1)S(1)}, bf16[4,112,448]{2,1,0:T(8,128)(2,1)}, u32[]{:S(2)}) copy-start(bf16[4,112,448]{2,1,0:T(8,128)(2,1)} %constant.77.clone.gather_ref) | copy-start | bytes 1204228
  311.1 5.6 %copy-start.11 = (bf16[256,896]{1,0:T(8,128)(2,1)S(1)}, bf16[256,896]{1,0:T(8,128)(2,1)}, u32[]{:S(2)}) copy-start(bf16[256,896]{1,0:T(8,128)(2,1)} %pad_maximum_fusion.2.weight_ref) | copy-start | bytes 1376260
  311.1 5.6 %copy-start.14 = (bf16[128,1024]{1,0:T(8,128)(2,1)S(1)}, bf16[128,1024]{1,0:T(8,128)(2,1)}, u32[]{:S(2)}) copy-start(bf16[128,1024]{1,0:T(8,128)(2,1)} %attention.1.rows_ref.base_ref) | copy-start | bytes 786436
  311.1 51.2 %all-to-all-start.3 = ((bf16[64,56,256]{2,1,0:T(8,128)(2,1)}), bf16[64,56,256]{2,1,0:T(8,128)(2,1)S(1)}, u32[]{:S(2)}, u32[]{:S(2)}) async-start(bf16[64,56,256]{2,1,0:T(8,128)(2,1)} %bitcast.27), calls=%async_computation.3 | async-start | bytes 3670016 | tf_op jit(solution)/shard_map/all_to_all | solution.py:311
  316.7 45.6 %copy-start.18 = (bf16[128,1024]{1,0:T(8,128)(2,1)S(1)}, bf16[128,1024]{1,0:T(8,128)(2,1)}, u32[]{:S(2)}) copy-start(bf16[128,1024]{1,0:T(8,128)(2,1)} %base_ref.1) | copy-start | bytes 786436
Sparse Core Ops, SparseCore 0:
  10.8 92.1 all-gather.1

commit v4 on v3

--- a/solution.py
+++ b/solution.py
@@ -55,7 +55,7 @@
     return lax.dot_general(a, b, (((1,), (1,)), ((), ())), preferred_element_type=F32)
 
 
-CHUNK = 8
+CHUNK = 16
 
 
 def attention_kernel(place_ref, q_ref, kv_ref, o_ref, q_s, m_s, l_s, acc_s):
@@ -172,7 +172,7 @@
             ).astype(BF16)
 
 
-TILE = 256
+TILE = 768
 
 
 def high_low(x):
@@ -220,7 +220,7 @@
             jax.ShapeDtypeStruct((PLACES, WIDTH), BF16),
             jax.ShapeDtypeStruct((PLACES, 128), BF16),
         ],
-        compiler_params=params(22),
+        compiler_params=params(30),
         name="first_product",
     )(x, gather, w)
 

time: 373 us -> 375 us (level); the launches traced: 372 us -> 368 us
  transfers between devices with their start and end apart: 18 -> 18, of which waited for: 13 -> 13; matrix products, arithmetic and copies ran while one was open for 5% -> 5% of each run, Pallas kernels for 5% -> 4%
where the time goes in v4:
time: 375 us; the launch traced here: 368 us
  waiting for transfers between devices  215 us (57%)
  starting transfers between devices  62.1 us (17%)
  Pallas kernels  40.6 us (11%)
  local copies, waits for them, and re-layouts  22 us (6%)
  between operations  15 us (4%)
  other arithmetic  12 us (3%)
    all_to_all x4, waiting for transfers between devices, exchange(): lax.all_to_all(x.reshape(EXPERTS, CAP * PIECES, PIECE), 'exp', split_axis...  134 us
    ppermute x13, waiting for transfers between devices, from_head(): lax.ppermute(x, 'head', [((i + d) % HEAD_COUNT, i) for i in range(HEAD_CO...  81.2 us
    all_to_all x4, starting transfers between devices, exchange(): lax.all_to_all(x.reshape(EXPERTS, CAP * PIECES, PIECE), 'exp', split_axis...  44 us
    ppermute x13, starting transfers between devices, from_head(): lax.ppermute(x, 'head', [((i + d) % HEAD_COUNT, i) for i in range(HEAD_CO...  18 us
    unnamed x60, local copies, waits for them, and re-layouts  14.9 us
    pallas_call x2, Pallas kernels, second_product(): pl.pallas_call(functools.partial(second_kernel, by_rows, rows is not None...  11.9 us
    pallas_call x2, Pallas kernels, first_product(): pl.pallas_call(functools.partial(first_kernel, by_rows), grid=(outs // TI...  8.96 us
  transfers between devices with their start and end apart: 18, of which 13 were waited for; matrix products, arithmetic and copies ran while one was open for 5% of the time, Pallas kernels for 4%

profile of v4, /device:TPU:2, one launch (start us, length us, event | category | flops | bytes accessed | tf_op | source)
XLA Modules:
  0.0 367.5 jit_solution(5055154456308219656)
XLA Ops:
  7.2 1.6 pad_maximum_fusion.3
  10.9 2.8 send_rows.2
  13.8 1.3 copy-done.1
  15.0 12.0 %all-to-all-start = ((bf16[64,56,256]{2,1,0:T(8,128)(2,1)}), bf16[64,56,256]{2,1,0:T(8,128)(2,1)S(1)}, u32[]{:S(2)}, u32[]{:S(2)}) async-start(bf16[64,56,256]{2,1,0:T(8,128)(2,1)} %bitcast.30), calls=%async_computation | async-start | bytes 3670016 | tf_op jit(solution)/shard_map/all_to_all | solution.py:311
  28.6 1.9 broadcast_in_dim.79
  30.5 2.0 copy.25
  32.5 1.8 fusion.2
  34.2 44.5 %all-to-all-done = bf16[64,56,256]{2,1,0:T(8,128)(2,1)S(1)} async-done(((bf16[64,56,256]{2,1,0:T(8,128)(2,1)}), bf16[64,56,256]{2,1,0:T(8,128)(2,1)S(1)}, u32[]{:S(2)}, u32[]{:S(2)}) %all-to-all-start) | async-done | bytes 1835040 | tf_op jit(solution)/shard_map/all_to_all | solution.py:311
  78.7 1.4 copy-done.9
  80.1 2.7 first_product.2
  83.7 2.8 collective-permute-start
  86.5 2.4 collective-permute-start.2
  89.8 11.0 %collective-permute-done = bf16[224,768]{1,0:T(8,128)(2,1)S(1)} collective-permute-done((bf16[224,768]{1,0:T(8,128)(2,1)S(1)}, bf16[224,768]{1,0:T(8,128)(2,1)S(1)}, u32[]{:S(2)}, u32[]{:S(2)}) %collective-permute-start) | collective-permute-done | bytes 344096 | tf_op jit(solution)/shard_map/ppermute | solution.py:318
  100.8 3.4 collective-permute-done.1
  104.9 6.4 %attention.1.rows_ref.base_ref = bf16[128,1024]{1,0:T(8,128)(2,1)} custom-call(s32[1]{0:T(128)} %bitcast.6.place_ref, bf16[128,1024]{1,0:T(8,128)(2,1)} %q_ref.1, bf16[8192,512]{1,0:T(8,128)(2,1)} %all-gather.2.cloned.1.call-done.kv_ref), custom_call_target="tpu_custom_call" | custom-call | tf_op jit(solution)/shard_map/attention/pallas_call | solution.py:123
  112.3 4.1 %send_rows.3 = bf16[3584,256]{1,0:T(8,128)(2,1)} custom-call(bf16[896,128]{1,0:T(8,128)(2,1)S(1)} %compare_convert_fusion.picker_ref, bf16[128,1024]{1,0:T(8,128)(2,1)S(1)} %copy-done.13, bf16[4,448,112]{2,1,0:T(8,128)(2,1)S(1)} %copy-done.6), custom_call_target="tpu_custom_call" | custom-call | tf_op jit(solution)/shard_map/send_rows/pallas_call | solution.py:158
  116.4 17.5 %all-to-all-start.1 = ((bf16[64,56,256]{2,1,0:T(8,128)(2,1)}), bf16[64,56,256]{2,1,0:T(8,128)(2,1)}, u32[]{:S(2)}, u32[]{:S(2)}) async-start(bf16[64,56,256]{2,1,0:T(8,128)(2,1)} %bitcast.7), calls=%async_computation.1 | async-start | bytes 3670016 | tf_op jit(solution)/shard_map/all_to_all | solution.py:311
  133.9 2.5 copy.27
  136.4 42.9 %all-to-all-done.1 = bf16[64,56,256]{2,1,0:T(8,128)(2,1)} async-done(((bf16[64,56,256]{2,1,0:T(8,128)(2,1)}), bf16[64,56,256]{2,1,0:T(8,128)(2,1)}, u32[]{:S(2)}, u32[]{:S(2)}) %all-to-all-start.1) | async-done | bytes 1835040 | tf_op jit(solution)/shard_map/all_to_all | solution.py:311
  180.3 6.3 %first_product.3 = (bf16[896,1536]{1,0:T(8,128)(2,1)S(1)}, bf16[896,1024]{1,0:T(8,128)(2,1)S(1)}, bf16[896,128]{1,0:T(8,128)(2,1)S(1)}) custom-call(bf16[3584,256]{1,0:T(8,128)(2,1)} %bitcast.8.x_ref, bf16[4,112,448]{2,1,0:T(8,128)(2,1)S(1)} %copy-done.4, bf16[1024,1536]{1,0:T(8,128)(2,1)S(1)} %bitcast.25), custom_call_target="tpu_custom_call" | custom-call | tf_op jit(solution)/shard_map/first_product/pallas_call | solution.py:205
  186.8 1.1 copy-done.15
  188.1 1.1 collective-permute-start.3
  189.1 1.0 collective-permute-start.4
  190.2 1.0 collective-permute-start.5
  191.2 16.5 %collective-permute-done.3 = bf16[224,1664]{1,0:T(8,128)(2,1)S(1)} collective-permute-done((bf16[224,1664]{1,0:T(8,128)(2,1)S(1)}, bf16[224,1664]{1,0:T(8,128)(2,1)S(1)}, u32[]{:S(2)}, u32[]{:S(2)}) %collective-permute-start.3) | collective-permute-done | bytes 745504 | tf_op jit(solution)/shard_map/ppermute | solution.py:318
  207.7 15.4 %collective-permute-done.4 = bf16[224,1664]{1,0:T(8,128)(2,1)S(1)} collective-permute-done((bf16[224,1664]{1,0:T(8,128)(2,1)S(1)}, bf16[224,1664]{1,0:T(8,128)(2,1)S(1)}, u32[]{:S(2)}, u32[]{:S(2)}) %collective-permute-start.4) | collective-permute-done | bytes 745504 | tf_op jit(solution)/shard_map/ppermute | solution.py:318
  223.7 2.8 add_reduce_fusion
  227.9 1.3 collective-permute-start.8
  230.1 1.3 convert_reduce_fusion
  231.5 2.0 pad_maximum_fusion.refs_0_
  233.5 6.3 %collective-permute-done.6.refs_1_ = bf16[224,768]{1,0:T(8,128)(2,1)} collective-permute-done((bf16[224,768]{1,0:T(8,128)(2,1)S(1)}, bf16[224,768]{1,0:T(8,128)(2,1)}, u32[]{:S(2)}, u32[]{:S(2)}) %collective-permute-start.6) | collective-permute-done | bytes 344096 | tf_op jit(solution)/shard_map/ppermute | solution.py:318
  239.9 3.7 %collective-permute-done.8.refs_3_ = bf16[224,768]{1,0:T(8,128)(2,1)} collective-permute-done((bf16[224,768]{1,0:T(8,128)(2,1)S(1)}, bf16[224,768]{1,0:T(8,128)(2,1)}, u32[]{:S(2)}, u32[]{:S(2)}) %collective-permute-start.8) | collective-permute-done | bytes 344096 | tf_op jit(solution)/shard_map/ppermute | solution.py:318
  243.6 1.4 copy-done.10
  245.0 5.7 %second_product.2 = bf16[3584,256]{1,0:T(8,128)(2,1)S(1)} custom-call(s32[1]{0:T(128)} %bitcast.head_ref, bf16[224,768]{1,0:T(8,128)(2,1)S(1)} %get-tuple-element.31.refs_0_, bf16[224,768]{1,0:T(8,128)(2,1)} %collective-permute-done.6.refs_1_, bf16[224,768]{1,0:T(8,128)(2,1)} %collective-permute-done.7.refs_2_, ...), custom_call_target="tpu_custom_call" | custom-call | tf_op jit(solution)/shard_map/second_product/pallas_call | solution.py:279
  250.7 1.3 copy-done.2
  252.0 8.8 %all-to-all-start.2 = ((bf16[64,56,256]{2,1,0:T(8,128)(2,1)}), bf16[64,56,256]{2,1,0:T(8,128)(2,1)}, u32[]{:S(2)}, u32[]{:S(2)}) async-start(bf16[64,56,256]{2,1,0:T(8,128)(2,1)} %bitcast.31), calls=%async_computation.2 | async-start | bytes 3670016 | tf_op jit(solution)/shard_map/all_to_all | solution.py:311
  261.1 3.2 collective-permute-start.9
  264.4 16.9 %collective-permute-done.10.refs_3_ = bf16[224,1664]{1,0:T(8,128)(2,1)S(1)} collective-permute-done((bf16[224,1664]{1,0:T(8,128)(2,1)}, bf16[224,1664]{1,0:T(8,128)(2,1)S(1)}, u32[]{:S(2)}, u32[]{:S(2)}) %collective-permute-start.10) | collective-permute-done | bytes 745504 | tf_op jit(solution)/shard_map/ppermute | solution.py:318
  281.4 3.3 collective-permute-start.12
  284.7 7.9 %collective-permute-done.11 = bf16[112,1664]{1,0:T(8,128)(2,1)S(1)} collective-permute-done((bf16[112,1664]{1,0:T(8,128)(2,1)S(1)}, bf16[112,1664]{1,0:T(8,128)(2,1)S(1)}, u32[]{:S(2)}, u32[]{:S(2)}) %collective-permute-start.11) | collective-permute-done | bytes 372768 | tf_op jit(solution)/shard_map/ppermute | solution.py:318
  292.7 1.5 copy-done.16
  294.2 6.2 %second_product.3 = bf16[3584,256]{1,0:T(8,128)(2,1)S(1)} custom-call(s32[1]{0:T(128)} %bitcast.head_ref, bf16[224,1664]{1,0:T(8,128)(2,1)S(1)} %copy-done.12, bf16[224,1664]{1,0:T(8,128)(2,1)S(1)} %collective-permute-done.9.refs_1_, bf16[224,1664]{1,0:T(8,128)(2,1)S(1)} %pad_maximum_fusion.1.refs_2_, bf16[224,1664]{1,0:T(8,128)(2,1)S(1)} %collective-permute-done.10.refs_3_, ...), custom_call_target="tpu_custom_call" | custom-call | tf_op jit(solution)/shard_map/second_product/pallas_call | solution.py:279
  300.4 1.2 copy-done
  301.7 4.7 %all-to-all-done.2 = bf16[64,56,256]{2,1,0:T(8,128)(2,1)} async-done(((bf16[64,56,256]{2,1,0:T(8,128)(2,1)}), bf16[64,56,256]{2,1,0:T(8,128)(2,1)}, u32[]{:S(2)}, u32[]{:S(2)}) %all-to-all-start.2) | async-done | bytes 1835040 | tf_op jit(solution)/shard_map/all_to_all | solution.py:311
  306.4 5.8 %all-to-all-start.3 = ((bf16[64,56,256]{2,1,0:T(8,128)(2,1)}), bf16[64,56,256]{2,1,0:T(8,128)(2,1)S(1)}, u32[]{:S(2)}, u32[]{:S(2)}) async-start(bf16[64,56,256]{2,1,0:T(8,128)(2,1)} %bitcast.27), calls=%async_computation.3 | async-start | bytes 3670016 | tf_op jit(solution)/shard_map/all_to_all | solution.py:311
  312.2 4.0 %combine.2 = bf16[128,1024]{1,0:T(8,128)(2,1)} custom-call(bf16[3584,256]{1,0:T(8,128)(2,1)} %bitcast.11.came_ref, bf16[4,112,448]{2,1,0:T(8,128)(2,1)S(1)} %copy-done.5, bf16[256,896]{1,0:T(8,128)(2,1)S(1)} %copy-done.11, bf16[128,1024]{1,0:T(8,128)(2,1)S(1)} %copy-done.14), custom_call_target="tpu_custom_call" | custom-call | tf_op jit(solution)/shard_map/combine/pallas_call | solution.py:301
  316.2 41.6 %all-to-all-done.3 = bf16[64,56,256]{2,1,0:T(8,128)(2,1)S(1)} async-done(((bf16[64,56,256]{2,1,0:T(8,128)(2,1)}), bf16[64,56,256]{2,1,0:T(8,128)(2,1)S(1)}, u32[]{:S(2)}, u32[]{:S(2)}) %all-to-all-start.3) | async-done | bytes 1835040 | tf_op jit(solution)/shard_map/all_to_all | solution.py:311
  357.8 2.5 combine.3
  (92 shorter events, 12.0 us)
Async XLA Ops:
  7.2 3.7 %copy-start.6 = (bf16[4,448,112]{2,1,0:T(8,128)(2,1)S(1)}, bf16[4,448,112]{2,1,0:T(8,128)(2,1)}, u32[]{:S(2)}) copy-start(bf16[4,448,112]{2,1,0:T(8,128)(2,1)} %constant.76.clone.spread_ref.refs_5_) | copy-start | bytes 1204228
  7.2 3.7 %copy-start.17 = (bf16[128,1024]{1,0:T(8,128)(2,1)S(1)}, bf16[128,1024]{1,0:T(8,128)(2,1)}, u32[]{:S(2)}) copy-start(bf16[128,1024]{1,0:T(8,128)(2,1)} %base_ref.1) | copy-start | bytes 786436
  7.2 97.8 %all-gather.2.cloned.1.call-start = ((), (), s32[]{:S(2)}) async-start(), calls=%async_computation.4 | async-start | bytes 8519680 | tf_op jit(solution)/shard_map/all_gather | solution.py:361
  13.8 1.3 copy-start.1
  15.0 63.7 %all-to-all-start = ((bf16[64,56,256]{2,1,0:T(8,128)(2,1)}), bf16[64,56,256]{2,1,0:T(8,128)(2,1)S(1)}, u32[]{:S(2)}, u32[]{:S(2)}) async-start(bf16[64,56,256]{2,1,0:T(8,128)(2,1)} %bitcast.30), calls=%async_computation | async-start | bytes 3670016 | tf_op jit(solution)/shard_map/all_to_all | solution.py:311
  27.0 0.7 copy-start.27
  27.1 0.7 copy-start.28
  27.7 50.9 %copy-start.3 = (bf16[4,112,448]{2,1,0:T(8,128)(2,1)S(1)}, bf16[4,112,448]{2,1,0:T(8,128)(2,1)}, u32[]{:S(2)}) copy-start(bf16[4,112,448]{2,1,0:T(8,128)(2,1)} %constant.77.clone.gather_ref) | copy-start | bytes 1204228
  78.7 1.5 copy-start.9
  82.8 6.1 %copy-start.20 = (f32[128,896]{1,0:T(8,128)S(1)}, f32[128,896]{1,0:T(8,128)}, u32[]{:S(2)}) copy-start(f32[128,896]{1,0:T(8,128)} %copy.25) | copy-start | bytes 1376260
  82.9 6.1 %copy-start.22 = (bf16[128,896]{1,0:T(8,128)(2,1)S(1)}, bf16[128,896]{1,0:T(8,128)(2,1)}, u32[]{:S(2)}) copy-start(bf16[128,896]{1,0:T(8,128)(2,1)} %fusion.2) | copy-start | bytes 688132
  83.7 17.1 %collective-permute-start = (bf16[224,768]{1,0:T(8,128)(2,1)S(1)}, bf16[224,768]{1,0:T(8,128)(2,1)S(1)}, u32[]{:S(2)}, u32[]{:S(2)}) collective-permute-start(bf16[224,768]{1,0:T(8,128)(2,1)S(1)} %get-tuple-element.49), channel_id=1, source_target_pairs={{1,0},{2,1},{3,2},{0,3},{5,4},{6,5},{7,6},{4,7},{9,8},{10,9},{11,1... | collective-permute-start | bytes 1032200 | tf_op jit(solution)/shard_map/ppermute | solution.py:318
  86.5 17.7 %collective-permute-start.1 = (bf16[224,768]{1,0:T(8,128)(2,1)S(1)}, bf16[224,768]{1,0:T(8,128)(2,1)S(1)}, u32[]{:S(2)}, u32[]{:S(2)}) collective-permute-start(bf16[224,768]{1,0:T(8,128)(2,1)S(1)} %get-tuple-element.48), channel_id=1, source_target_pairs={{3,0},{0,1},{1,2},{2,3},{7,4},{4,5},{5,6},{6,7},{11,8},{8,9},{9,10... | collective-permute-start | bytes 1032200 | tf_op jit(solution)/shard_map/ppermute | solution.py:318
  86.5 18.5 %collective-permute-start.2 = (bf16[224,768]{1,0:T(8,128)(2,1)S(1)}, bf16[224,768]{1,0:T(8,128)(2,1)}, u32[]{:S(2)}, u32[]{:S(2)}) collective-permute-start(bf16[224,768]{1,0:T(8,128)(2,1)S(1)} %get-tuple-element.47), channel_id=1, source_target_pairs={{2,0},{3,1},{0,2},{1,3},{6,4},{7,5},{4,6},{5,7},{10,8},{11,9},{8,1... | collective-permute-start | bytes 1032200 | tf_op jit(solution)/shard_map/ppermute | solution.py:318
  100.8 3.4 copy-start.23
  104.2 0.7 copy-start.25
  111.4 0.9 copy-start.13
  116.4 62.9 %all-to-all-start.1 = ((bf16[64,56,256]{2,1,0:T(8,128)(2,1)}), bf16[64,56,256]{2,1,0:T(8,128)(2,1)}, u32[]{:S(2)}, u32[]{:S(2)}) async-start(bf16[64,56,256]{2,1,0:T(8,128)(2,1)} %bitcast.7), calls=%async_computation.1 | async-start | bytes 3670016 | tf_op jit(solution)/shard_map/all_to_all | solution.py:311
  179.3 1.0 copy-start.4
  186.6 1.3 copy-start.15
  188.1 19.7 %collective-permute-start.3 = (bf16[224,1664]{1,0:T(8,128)(2,1)S(1)}, bf16[224,1664]{1,0:T(8,128)(2,1)S(1)}, u32[]{:S(2)}, u32[]{:S(2)}) collective-permute-start(bf16[224,1664]{1,0:T(8,128)(2,1)S(1)} %get-tuple-element.43), channel_id=1, source_target_pairs={{1,0},{2,1},{3,2},{0,3},{5,4},{6,5},{7,6},{4,7},{9,8},{10,9},{11,1... | collective-permute-start | bytes 2236424 | tf_op jit(solution)/shard_map/ppermute | solution.py:318
  189.1 34.0 %collective-permute-start.4 = (bf16[224,1664]{1,0:T(8,128)(2,1)S(1)}, bf16[224,1664]{1,0:T(8,128)(2,1)S(1)}, u32[]{:S(2)}, u32[]{:S(2)}) collective-permute-start(bf16[224,1664]{1,0:T(8,128)(2,1)S(1)} %get-tuple-element.45), channel_id=1, source_target_pairs={{3,0},{0,1},{1,2},{2,3},{7,4},{4,5},{5,6},{6,7},{11,8},{8,9},{9,10... | collective-permute-start | bytes 2236424 | tf_op jit(solution)/shard_map/ppermute | solution.py:318
  190.2 33.0 %collective-permute-start.5 = (bf16[224,1664]{1,0:T(8,128)(2,1)S(1)}, bf16[224,1664]{1,0:T(8,128)(2,1)S(1)}, u32[]{:S(2)}, u32[]{:S(2)}) collective-permute-start(bf16[224,1664]{1,0:T(8,128)(2,1)S(1)} %get-tuple-element.44), channel_id=1, source_target_pairs={{2,0},{3,1},{0,2},{1,3},{6,4},{7,5},{4,6},{5,7},{10,8},{11,9},{8,1... | collective-permute-start | bytes 2236424 | tf_op jit(solution)/shard_map/ppermute | solution.py:318
  191.2 32.5 %copy-start.21 = (bf16[224,768]{1,0:T(8,128)(2,1)S(1)}, bf16[224,768]{1,0:T(8,128)(2,1)}, u32[]{:S(2)}) copy-start(bf16[224,768]{1,0:T(8,128)(2,1)} %get-tuple-element.24) | copy-start | bytes 1032196
  191.2 32.5 %copy-start.24 = (bf16[224,768]{1,0:T(8,128)(2,1)S(1)}, bf16[224,768]{1,0:T(8,128)(2,1)}, u32[]{:S(2)}) copy-start(bf16[224,768]{1,0:T(8,128)(2,1)} %copy-done.23) | copy-start | bytes 1032196
  191.2 32.5 %copy-start.26 = (bf16[224,768]{1,0:T(8,128)(2,1)S(1)}, bf16[224,768]{1,0:T(8,128)(2,1)}, u32[]{:S(2)}) copy-start(bf16[224,768]{1,0:T(8,128)(2,1)} %copy-done.25) | copy-start | bytes 1032196
  223.5 3.0 copy-start.19
  226.5 13.3 %collective-permute-start.6 = (bf16[224,768]{1,0:T(8,128)(2,1)S(1)}, bf16[224,768]{1,0:T(8,128)(2,1)}, u32[]{:S(2)}, u32[]{:S(2)}) collective-permute-start(bf16[224,768]{1,0:T(8,128)(2,1)S(1)} %get-tuple-element.31.refs_0_), channel_id=1, source_target_pairs={{1,0},{2,1},{3,2},{0,3},{5,4},{6,5},{7,6},{4,7},{9,8},{10,9},{11,1... | collective-permute-start | bytes 1032200 | tf_op jit(solution)/shard_map/ppermute | solution.py:318
  227.3 12.6 %collective-permute-start.7 = (bf16[224,768]{1,0:T(8,128)(2,1)S(1)}, bf16[224,768]{1,0:T(8,128)(2,1)}, u32[]{:S(2)}, u32[]{:S(2)}) collective-permute-start(bf16[224,768]{1,0:T(8,128)(2,1)S(1)} %get-tuple-element.31.refs_0_), channel_id=1, source_target_pairs={{2,0},{3,1},{0,2},{1,3},{6,4},{7,5},{4,6},{5,7},{10,8},{11,9},{8,1... | collective-permute-start | bytes 1032200 | tf_op jit(solution)/shard_map/ppermute | solution.py:318
  227.9 15.7 %collective-permute-start.8 = (bf16[224,768]{1,0:T(8,128)(2,1)S(1)}, bf16[224,768]{1,0:T(8,128)(2,1)}, u32[]{:S(2)}, u32[]{:S(2)}) collective-permute-start(bf16[224,768]{1,0:T(8,128)(2,1)S(1)} %get-tuple-element.31.refs_0_), channel_id=1, source_target_pairs={{3,0},{0,1},{1,2},{2,3},{7,4},{4,5},{5,6},{6,7},{11,8},{8,9},{9,10... | collective-permute-start | bytes 1032200 | tf_op jit(solution)/shard_map/ppermute | solution.py:318
  230.0 13.6 %copy-start.7 = (bf16[4,448,112]{2,1,0:T(8,128)(2,1)S(1)}, bf16[4,448,112]{2,1,0:T(8,128)(2,1)}, u32[]{:S(2)}) copy-start(bf16[4,448,112]{2,1,0:T(8,128)(2,1)} %constant.76.clone.spread_ref.refs_5_) | copy-start | bytes 1204228
  243.6 1.4 copy-start.10
  250.7 1.3 copy-start.2
  252.0 54.4 %all-to-all-start.2 = ((bf16[64,56,256]{2,1,0:T(8,128)(2,1)}), bf16[64,56,256]{2,1,0:T(8,128)(2,1)}, u32[]{:S(2)}, u32[]{:S(2)}) async-start(bf16[64,56,256]{2,1,0:T(8,128)(2,1)} %bitcast.31), calls=%async_computation.2 | async-start | bytes 3670016 | tf_op jit(solution)/shard_map/all_to_all | solution.py:311
  260.8 31.9 %copy-start.8 = (bf16[4,448,112]{2,1,0:T(8,128)(2,1)S(1)}, bf16[4,448,112]{2,1,0:T(8,128)(2,1)}, u32[]{:S(2)}) copy-start(bf16[4,448,112]{2,1,0:T(8,128)(2,1)} %constant.76.clone.spread_ref.refs_5_) | copy-start | bytes 1204228
  260.8 31.9 %copy-start.12 = (bf16[224,1664]{1,0:T(8,128)(2,1)S(1)}, bf16[224,1664]{1,0:T(8,128)(2,1)}, u32[]{:S(2)}) copy-start(bf16[224,1664]{1,0:T(8,128)(2,1)} %pad_maximum_fusion.refs_0_) | copy-start | bytes 2236420
  260.8 20.5 %collective-permute-start.10 = (bf16[224,1664]{1,0:T(8,128)(2,1)}, bf16[224,1664]{1,0:T(8,128)(2,1)S(1)}, u32[]{:S(2)}, u32[]{:S(2)}) collective-permute-start(bf16[224,1664]{1,0:T(8,128)(2,1)} %pad_maximum_fusion.refs_0_), channel_id=1, source_target_pairs={{3,0},{0,1},{1,2},{2,3},{7,4},{4,5},{5,6},{6,7},{11,8},{8,9},{9,10... | collective-permute-start | bytes 2236424 | tf_op jit(solution)/shard_map/ppermute | solution.py:318
  261.1 20.3 %collective-permute-start.9 = (bf16[224,1664]{1,0:T(8,128)(2,1)}, bf16[224,1664]{1,0:T(8,128)(2,1)S(1)}, u32[]{:S(2)}, u32[]{:S(2)}) collective-permute-start(bf16[224,1664]{1,0:T(8,128)(2,1)} %pad_maximum_fusion.refs_0_), channel_id=1, source_target_pairs={{1,0},{2,1},{3,2},{0,3},{5,4},{6,5},{7,6},{4,7},{9,8},{10,9},{11,1... | collective-permute-start | bytes 2236424 | tf_op jit(solution)/shard_map/ppermute | solution.py:318
  281.3 11.3 %collective-permute-start.11 = (bf16[112,1664]{1,0:T(8,128)(2,1)S(1)}, bf16[112,1664]{1,0:T(8,128)(2,1)S(1)}, u32[]{:S(2)}, u32[]{:S(2)}) collective-permute-start(bf16[112,1664]{1,0:T(8,128)(2,1)S(1)} %slice.28), channel_id=1, source_target_pairs={{3,0},{0,1},{1,2},{2,3},{7,4},{4,5},{5,6},{6,7},{11,8},{8,9},{9,10... | collective-permute-start | bytes 1118216 | tf_op jit(solution)/shard_map/ppermute | solution.py:318
  281.4 11.2 %collective-permute-start.12 = (bf16[112,1664]{1,0:T(8,128)(2,1)S(1)}, bf16[112,1664]{1,0:T(8,128)(2,1)S(1)}, u32[]{:S(2)}, u32[]{:S(2)}) collective-permute-start(bf16[112,1664]{1,0:T(8,128)(2,1)S(1)} %slice.29), channel_id=1, source_target_pairs={{1,0},{2,1},{3,2},{0,3},{5,4},{6,5},{7,6},{4,7},{9,8},{10,9},{11,1... | collective-permute-start | bytes 1118216 | tf_op jit(solution)/shard_map/ppermute | solution.py:318
  292.7 1.5 copy-start.16
  300.4 1.3 copy-start
  306.4 5.8 %copy-start.5 = (bf16[4,112,448]{2,1,0:T(8,128)(2,1)S(1)}, bf16[4,112,448]{2,1,0:T(8,128)(2,1)}, u32[]{:S(2)}) copy-start(bf16[4,112,448]{2,1,0:T(8,128)(2,1)} %constant.77.clone.gather_ref) | copy-start | bytes 1204228
  306.4 5.8 %copy-start.11 = (bf16[256,896]{1,0:T(8,128)(2,1)S(1)}, bf16[256,896]{1,0:T(8,128)(2,1)}, u32[]{:S(2)}) copy-start(bf16[256,896]{1,0:T(8,128)(2,1)} %pad_maximum_fusion.2.weight_ref) | copy-start | bytes 1376260
  306.4 5.8 %copy-start.14 = (bf16[128,1024]{1,0:T(8,128)(2,1)S(1)}, bf16[128,1024]{1,0:T(8,128)(2,1)}, u32[]{:S(2)}) copy-start(bf16[128,1024]{1,0:T(8,128)(2,1)} %attention.1.rows_ref.base_ref) | copy-start | bytes 786436
  306.4 51.4 %all-to-all-start.3 = ((bf16[64,56,256]{2,1,0:T(8,128)(2,1)}), bf16[64,56,256]{2,1,0:T(8,128)(2,1)S(1)}, u32[]{:S(2)}, u32[]{:S(2)}) async-start(bf16[64,56,256]{2,1,0:T(8,128)(2,1)} %bitcast.27), calls=%async_computation.3 | async-start | bytes 3670016 | tf_op jit(solution)/shard_map/all_to_all | solution.py:311
  312.1 45.6 %copy-start.18 = (bf16[128,1024]{1,0:T(8,128)(2,1)S(1)}, bf16[128,1024]{1,0:T(8,128)(2,1)}, u32[]{:S(2)}) copy-start(bf16[128,1024]{1,0:T(8,128)(2,1)} %base_ref.1) | copy-start | bytes 786436
Sparse Core Ops, SparseCore 0:
  10.8 92.1 all-gather.1
